TPU v7x, 256 devices: a whole 4x4x8 slice. The times are simulated.
256 devices in a mesh: row: 16 (over x, y), col: 16 (over z, core).
Axes of the slice: x: 4, y: 4, z: 8, core: 2. Of those that a mesh axis runs over, the one named last changes fastest.
Arguments:
- activations: bfloat16 [2048, 16384], P('col', 'row'), may hold values from -6 to 6
- grad_output: bfloat16 [2048, 16384], P('col', 'row'), may hold values from -6 to 6
- gate_pre: bfloat16 [2048, 8192], P('row', 'col'), may hold values from -8 to 8
- up_pre: bfloat16 [2048, 8192], P('row', 'col'), may hold values from -6 to 6
- w_gate: bfloat16 [16384, 8192], P('row', 'col'), may hold values from -0.046875 to 0.046875
- w_up: bfloat16 [16384, 8192], P('row', 'col'), may hold values from -0.046875 to 0.046875
- w_down: bfloat16 [8192, 16384], P('col', 'row'), may hold values from -0.0625 to 0.0625
Outputs:
- grad_input: bfloat16 [2048, 16384], P('col', 'row')
- grad_gate: bfloat16 [16384, 8192], P('row', 'col')
- grad_up: bfloat16 [16384, 8192], P('row', 'col')
- grad_down: bfloat16 [8192, 16384], P('col', 'row')
All inputs are finite; a program needn't handle non-finite values.
Results may differ from a plain program's by a relative error of at most 0.005.
Values may be sent and summed in bfloat16 or wider, within the bound.
No kernel may reach another device: no remote copies, remote signals or barrier semaphores. Data moves between devices by JAX's collectives and lax.ppermute only.
A program may use at most 128 MiB of HBM per device.

v0:
```python
import jax
import jax.numpy as jnp
from jax import lax
from jax.sharding import PartitionSpec as P


def swiglu_grads(grad_hidden, gate_pre, up_pre):
    gate_val = gate_pre.astype(jnp.float32)
    up_val = up_pre.astype(jnp.float32)
    sigma = 1.0 / (1.0 + jnp.exp(-gate_val))
    grad_gate_pre = (grad_hidden * up_val * sigma * (1.0 + gate_val * (1.0 - sigma))).astype(
        jnp.bfloat16
    )
    grad_up_pre = (grad_hidden * gate_val * sigma).astype(jnp.bfloat16)
    return (grad_gate_pre, grad_up_pre)


def hidden_value(gate_pre, up_pre):
    gate_val = gate_pre.astype(jnp.float32)
    sigma = 1.0 / (1.0 + jnp.exp(-gate_val))
    return (gate_val * sigma * up_pre.astype(jnp.float32)).astype(jnp.bfloat16)


def local(activations, grad_output, gate_pre, up_pre, w_gate, w_up, w_down):
    contract_cols = (((1,), (1,)), ((), ()))
    contract_rows = (((0,), (0,)), ((), ()))
    acts_whole, grad_whole = (
        lax.all_gather(activations, "col", axis=0, tiled=True),
        lax.all_gather(grad_output, "col", axis=0, tiled=True),
    )
    hidden_local = hidden_value(gate_pre, up_pre)
    hidden_all = lax.all_gather(hidden_local, "row", axis=0, tiled=True)
    grad_hidden = lax.psum_scatter(
        lax.dot_general(grad_whole, w_down, contract_cols, preferred_element_type=jnp.float32),
        "row",
        scatter_dimension=0,
        tiled=True,
    )
    gate_grad_local, up_grad_local = swiglu_grads(grad_hidden, gate_pre, up_pre)
    gate_grad_all, up_grad_all = (
        lax.all_gather(gate_grad_local, "row", axis=0, tiled=True),
        lax.all_gather(up_grad_local, "row", axis=0, tiled=True),
    )
    grad_down = lax.dot_general(
        hidden_all, grad_whole, contract_rows, preferred_element_type=jnp.float32
    ).astype(jnp.bfloat16)
    grad_gate = lax.dot_general(
        acts_whole, gate_grad_all, contract_rows, preferred_element_type=jnp.float32
    ).astype(jnp.bfloat16)
    grad_up = lax.dot_general(
        acts_whole, up_grad_all, contract_rows, preferred_element_type=jnp.float32
    ).astype(jnp.bfloat16)
    total = lax.dot_general(
        gate_grad_all, w_gate, contract_cols, preferred_element_type=jnp.float32
    )
    grad_input = lax.psum_scatter(
        total
        + lax.dot_general(up_grad_all, w_up, contract_cols, preferred_element_type=jnp.float32),
        "col",
        scatter_dimension=0,
        tiled=True,
    ).astype(jnp.bfloat16)
    return (grad_input, grad_gate, grad_up, grad_down)


def solution(mesh):
    in_specs = (
        P("col", "row"),
        P("col", "row"),
        P("row", "col"),
        P("row", "col"),
        P("row", "col"),
        P("row", "col"),
        P("col", "row"),
    )
    out_specs = (P("col", "row"), P("row", "col"), P("row", "col"), P("col", "row"))
    return jax.shard_map(local, mesh=mesh, in_specs=in_specs, out_specs=out_specs, check_vma=False)
```

profile of v0, /device:TPU:1, one launch (start us, length us, event | category | flops | bytes accessed | tf_op | source)
XLA Modules:
  0.0 422.3 jit_solution(2500429104871966908)
XLA Ops:
  7.2 0.0 copy-start
  7.2 0.0 all-gather.6.cloned.1.call-start
  7.2 0.7 all-gather.6.cloned.1.call-update
  7.9 0.0 reduce-scatter.3.cloned.1.call-start
  8.0 48.2 %all-gather.6.cloned.1.call-done = bf16[2048,1024]{1,0:T(8,128)(2,1)} async-done(((bf16[128,1024]{1,0:T(8,128)(2,1)}), bf16[2048,1024]{1,0:T(8,128)(2,1)}) %all-gather.6.cloned.1.call-update) | async-done | bytes 4194320 | tf_op jit(solution)/shard_map/all_gather | solution.py:29
  56.2 6.8 %fusion.12 = f32[2048,512]{1,0:T(8,128)} fusion(bf16[2048,1024]{1,0:T(8,128)(2,1)} %all-gather.6.cloned.1.call-done, bf16[512,1024]{1,0:T(8,128)(2,1)} %param.13), kind=kOutput, calls=%fused_computation.22 | convolution fusion | flops 2147483648 | bytes 9437184 | tf_op jit(solution)/shard_map/dot_general | solution.py:34
  63.0 0.0 reduce-scatter.3.cloned.1.call-update
  63.0 0.0 all-gather.8.cloned.1.call-start
  63.1 79.2 %reduce-scatter.3.cloned.1.call-done = f32[128,512]{1,0:T(8,128)} async-done(((f32[2048,512]{1,0:T(8,128)}), f32[128,512]{1,0:T(8,128)}) %reduce-scatter.3.cloned.1.call-update) | async-done | bytes 262160 | tf_op jit(solution)/shard_map/reduce_scatter | solution.py:33
  142.3 1.8 fusion.11
  144.2 0.0 all-gather.8.cloned.1.call-update
  144.2 0.0 all-gather.10.cloned.1.call-start
  144.2 0.5 all-gather.10.cloned.1.call-update
  144.8 0.0 all-gather.12.cloned.1.call-start
  144.8 0.5 all-gather.12.cloned.1.call-update
  145.4 0.0 all-gather.14.cloned.1.call-start
  145.4 0.5 all-gather.14.cloned.1.call-update
  146.0 0.2 reduce-scatter.5.cloned.1.call-start
  146.2 49.7 %all-gather.8.cloned.1.call-done = bf16[2048,512]{1,0:T(8,128)(2,1)} async-done(((bf16[128,512]{1,0:T(8,128)(2,1)}), bf16[2048,512]{1,0:T(8,128)(2,1)}) %all-gather.8.cloned.1.call-update) | async-done | bytes 2097168 | tf_op jit(solution)/shard_map/all_gather | solution.py:41
  195.9 7.2 %fusion.13 = f32[2048,1024]{1,0:T(8,128)} fusion(bf16[2048,512]{1,0:T(8,128)(2,1)} %all-gather.8.cloned.1.call-done, bf16[1024,512]{1,0:T(8,128)(2,1)S(1)} %copy-done), kind=kOutput, calls=%fused_computation.23 | convolution fusion | flops 2147483648 | bytes 11534336 | tf_op jit(solution)/shard_map/dot_general | solution.py:53
  203.1 45.3 %all-gather.10.cloned.1.call-done = bf16[2048,512]{1,0:T(8,128)(2,1)} async-done(((bf16[128,512]{1,0:T(8,128)(2,1)}), bf16[2048,512]{1,0:T(8,128)(2,1)}) %all-gather.10.cloned.1.call-update) | async-done | bytes 2097168 | tf_op jit(solution)/shard_map/all_gather | solution.py:42
  248.4 9.6 %convolution_add_fusion = f32[2048,1024]{1,0:T(8,128)} fusion(f32[2048,1024]{1,0:T(8,128)} %fusion.13, bf16[2048,512]{1,0:T(8,128)(2,1)} %all-gather.10.cloned.1.call-done, bf16[1024,512]{1,0:T(8,128)(2,1)S(1)} %copy-done.2), kind=kOutput, calls=%fused_computation | convolution fusion | flops 2149580800 | bytes 19922944 | tf_op jit(solution)/shard_map/dot_general | solution.py:58
  258.1 0.0 reduce-scatter.5.cloned.1.call-update
  258.1 35.0 %all-gather.12.cloned.1.call-done = bf16[2048,1024]{1,0:T(8,128)(2,1)} async-done(((bf16[128,1024]{1,0:T(8,128)(2,1)}), bf16[2048,1024]{1,0:T(8,128)(2,1)}) %all-gather.12.cloned.1.call-update) | async-done | bytes 4194320 | tf_op jit(solution)/shard_map/all_gather | solution.py:28
  293.0 5.5 %fusion.1 = bf16[1024,512]{0,1:T(8,128)(2,1)} fusion(bf16[2048,512]{1,0:T(8,128)(2,1)S(1)} %copy-done.1, bf16[2048,1024]{1,0:T(8,128)(2,1)} %all-gather.12.cloned.1.call-done), kind=kOutput, calls=%fused_computation.5 | convolution fusion | flops 2148007936 | bytes 7340032 | tf_op jit(solution)/shard_map/dot_general | solution.py:50
  298.5 2.3 copy.12
  300.8 5.2 %fusion = bf16[1024,512]{0,1:T(8,128)(2,1)S(1)} fusion(bf16[2048,512]{1,0:T(8,128)(2,1)} %all-gather.8.cloned.1.call-done, bf16[2048,1024]{1,0:T(8,128)(2,1)} %all-gather.12.cloned.1.call-done), kind=kOutput, calls=%fused_computation.4 | convolution fusion | flops 2148007936 | bytes 7340032 | tf_op jit(solution)/shard_map/dot_general | solution.py:47
  306.0 1.3 copy.11
  307.3 35.6 %all-gather.14.cloned.1.call-done = bf16[2048,512]{1,0:T(8,128)(2,1)} async-done(((bf16[128,512]{1,0:T(8,128)(2,1)}), bf16[2048,512]{1,0:T(8,128)(2,1)}) %all-gather.14.cloned.1.call-update) | async-done | bytes 2097168 | tf_op jit(solution)/shard_map/all_gather | solution.py:32
  342.9 6.1 %convolution_convert_fusion = bf16[512,1024]{1,0:T(8,128)(2,1)} fusion(bf16[2048,512]{1,0:T(8,128)(2,1)} %all-gather.14.cloned.1.call-done, bf16[2048,1024]{1,0:T(8,128)(2,1)} %all-gather.6.cloned.1.call-done), kind=kOutput, calls=%fused_computation.1 | convolution fusion | flops 2148007936 | bytes 7340032 | tf_op jit(solution)/shard_map/dot_general | solution.py:44
  349.1 64.6 %reduce-scatter.5.cloned.1.call-done = f32[128,1024]{1,0:T(8,128)} async-done(((f32[2048,1024]{1,0:T(8,128)}), f32[128,1024]{1,0:T(8,128)}) %reduce-scatter.5.cloned.1.call-update) | async-done | bytes 524304 | tf_op jit(solution)/shard_map/reduce_scatter | solution.py:56
  413.6 1.8 convert_element_type.39
  (9 shorter events, 0.0 us)
Async XLA Ops:
  7.2 188.7 %copy-start = (bf16[1024,512]{1,0:T(8,128)(2,1)S(1)}, bf16[1024,512]{1,0:T(8,128)(2,1)}, u32[]{:S(2)}) copy-start(bf16[1024,512]{1,0:T(8,128)(2,1)} %param.11) | copy-start | bytes 3145732
  7.2 49.0 %all-gather.6.cloned.1.call-start = ((), (), s32[]{:S(2)}) async-start(), calls=%async_computation.2 | async-start | bytes 4456448 | tf_op jit(solution)/shard_map/all_gather | solution.py:29
  7.9 134.4 %reduce-scatter.3.cloned.1.call-start = ((), (), s32[]{:S(2)}) async-start(), calls=%async_computation.3 | async-start | bytes 4456448 | tf_op jit(solution)/shard_map/reduce_scatter | solution.py:33
  63.0 79.3 %copy-start.3 = (bf16[128,512]{1,0:T(8,128)(2,1)S(1)}, bf16[128,512]{1,0:T(8,128)(2,1)}, u32[]{:S(2)}) copy-start(bf16[128,512]{1,0:T(8,128)(2,1)} %param.9) | copy-start | bytes 393220
  63.0 79.3 %copy-start.4 = (bf16[128,512]{1,0:T(8,128)(2,1)S(1)}, bf16[128,512]{1,0:T(8,128)(2,1)}, u32[]{:S(2)}) copy-start(bf16[128,512]{1,0:T(8,128)(2,1)} %param.10) | copy-start | bytes 393220
  63.0 132.8 %all-gather.8.cloned.1.call-start = ((), (), s32[]{:S(2)}) async-start(), calls=%async_computation.4 | async-start | bytes 2228224 | tf_op jit(solution)/shard_map/all_gather | solution.py:41
  144.2 104.2 %all-gather.10.cloned.1.call-start = ((), (), s32[]{:S(2)}) async-start(), calls=%async_computation.5 | async-start | bytes 2228224 | tf_op jit(solution)/shard_map/all_gather | solution.py:42
  144.8 148.3 %all-gather.12.cloned.1.call-start = ((), (), s32[]{:S(2)}) async-start(), calls=%async_computation.7 | async-start | bytes 4456448 | tf_op jit(solution)/shard_map/all_gather | solution.py:28
  145.4 197.6 %all-gather.14.cloned.1.call-start = ((), (), s32[]{:S(2)}) async-start(), calls=%async_computation.8 | async-start | bytes 2228224 | tf_op jit(solution)/shard_map/all_gather | solution.py:32
  145.9 102.5 %copy-start.2 = (bf16[1024,512]{1,0:T(8,128)(2,1)S(1)}, bf16[1024,512]{1,0:T(8,128)(2,1)}, u32[]{:S(2)}) copy-start(bf16[1024,512]{1,0:T(8,128)(2,1)} %param.12) | copy-start | bytes 3145732
  146.0 267.7 %reduce-scatter.5.cloned.1.call-start = ((), (), s32[]{:S(2)}) async-start(), calls=%async_computation.6 | async-start | bytes 8912896 | tf_op jit(solution)/shard_map/reduce_scatter | solution.py:56
  258.0 35.0 %copy-start.1 = (bf16[2048,512]{1,0:T(8,128)(2,1)S(1)}, bf16[2048,512]{1,0:T(8,128)(2,1)}, u32[]{:S(2)}) copy-start(bf16[2048,512]{1,0:T(8,128)(2,1)} %all-gather.10.cloned.1.call-done) | copy-start | bytes 6291460
Sparse Core Ops, SparseCore 0:
  9.8 46.3 all-gather.5
  63.2 79.1 reduce-scatter.2
  145.6 50.1 all-gather.7
  199.0 49.3 all-gather.9
  250.2 42.7 all-gather.11
  295.6 47.2 all-gather.13
  345.6 67.9 reduce-scatter.4
where the time goes:
time: 425 us; the launch traced here: 422 us
  waiting for transfers between devices  360 us (85%)
  matrix products  40.5 us (10%)
  between operations  14.2 us (3%)
    reduce_scatter x1, waiting for transfers between devices, local(): lax.psum_scatter(lax.dot_general(grad_whole, w_down, contract_cols, prefe...  79.2 us
    reduce_scatter x1, waiting for transfers between devices, local(): lax.psum_scatter(total + lax.dot_general(up_grad_all, w_up, contract_cols...  64.6 us
    all_gather x1, waiting for transfers between devices, local(): lax.all_gather(gate_grad_local, 'row', axis=0, tiled=True)  49.7 us
    all_gather x1, waiting for transfers between devices, local(): lax.all_gather(grad_output, 'col', axis=0, tiled=True)  48.2 us
    all_gather x1, waiting for transfers between devices, local(): lax.all_gather(up_grad_local, 'row', axis=0, tiled=True)  45.3 us
    all_gather x1, waiting for transfers between devices, local(): hidden_all = lax.all_gather(hidden_local, 'row', axis=0, tiled=True)  35.6 us
    all_gather x1, waiting for transfers between devices, local(): lax.all_gather(activations, 'col', axis=0, tiled=True)  35 us
    dot_general x1, matrix products, local(): lax.dot_general(up_grad_all, w_up, contract_cols, preferred_element_type=...  9.64 us
  transfers between devices with their start and end apart: 7, of which 7 were waited for; matrix products, arithmetic and copies ran while one was open for 9% of the time, Pallas kernels for 0%

commit v1 on v0

v1 whole, which is shorter than its diff:
```python
import jax
import jax.numpy as jnp
from jax import lax
from jax.experimental import pallas as pl
from jax.experimental.pallas import tpu as pltpu
from jax.sharding import Mesh, PartitionSpec as P

AXES = ("x", "y", "z", "core")
DIMS = (4, 4, 8, 2)
F32 = jnp.float32
BF16 = jnp.bfloat16


def device_pairs(target):
    def number(x, y, z, k):
        return ((x % 4 * 4 + y % 4) * 8 + z % 8) * 2 + k % 2

    return [
        (number(x, y, z, k), number(*target(x, y, z, k)))
        for x in range(4)
        for y in range(4)
        for z in range(8)
        for k in range(2)
    ]


def send(value, target):
    return lax.ppermute(value, AXES, device_pairs(target))


def round_z(value):
    return send(value, lambda x, y, z, k: (x, y, z + 1 - 2 * k, k))


def other_core(value):
    return send(value, lambda x, y, z, k: (x, y, z, k + 1))


def along_a(value, step):
    return send(
        value,
        lambda x, y, z, k: (x + step, y, z, k) if k == 0 else (x, y + step, z, k),
    )


def along_b(value, step):
    return send(
        value,
        lambda x, y, z, k: (x, y + step, z, k) if k == 0 else (x + step, y, z, k),
    )


def gather_rows(value):
    got = {0: value}
    for step in (2, 1, 3):
        got[(-step) % 4] = along_b(value, step)
    line = jnp.concatenate([got[i] for i in range(4)], axis=0)
    got = {0: line}
    for step in (2, 1, 3):
        got[(-step) % 4] = along_a(line, step)
    return [got[i] for i in range(4)]


def join(*values):
    return lax.optimization_barrier(values)


def pair_product(order, *refs):
    out = refs[-1]
    total = None
    for i in range(0, len(refs) - 1, 3):
        first, second, weights = refs[i : i + 3]
        both = jnp.concatenate([first[...], second[...]], axis=0)
        part = lax.dot_general(
            both, weights[...], (((1,), (1,)), ((), ())), preferred_element_type=F32
        )
        total = part if total is None else total + part
    out[...] = total.astype(out.dtype)


def block_product(terms, order, dtype):
    n = order.shape[0]
    rows = terms[0][0].shape[0] // 16
    width, depth = terms[0][1].shape
    specs, operands = [], []
    for value, weights in terms:
        specs += [
            pl.BlockSpec((rows, depth), lambda i, at: (at[2 * i], 0)),
            pl.BlockSpec((rows, depth), lambda i, at: (at[2 * i + 1], 0)),
            pl.BlockSpec((width, depth), lambda i, at: (0, 0)),
        ]
        operands += [value, value, weights]
    grid_spec = pltpu.PrefetchScalarGridSpec(
        num_scalar_prefetch=1,
        grid=(n // 2,),
        in_specs=specs,
        out_specs=pl.BlockSpec((2 * rows, width), lambda i, at: (i, 0)),
    )
    return pl.pallas_call(
        pair_product,
        grid_spec=grid_spec,
        out_shape=jax.ShapeDtypeStruct((n * rows, width), dtype),
        compiler_params=pltpu.CompilerParams(vmem_limit_bytes=32 * 1024 * 1024),
        cost_estimate=pl.CostEstimate(
            flops=2 * len(terms) * n * rows * width * depth,
            bytes_accessed=2 * len(terms) * (n * rows + width) * depth
            + n * rows * width * jnp.dtype(dtype).itemsize,
            transcendentals=0,
        ),
    )(order, *operands)


def swiglu_hidden(order, pre_ref, *refs):
    out = refs[-1]
    ff = out.shape[1]
    gate_val = pre_ref[:, :ff].astype(F32)
    up_val = pre_ref[:, ff:].astype(F32)
    sigma = 1.0 / (1.0 + jnp.exp(-gate_val))
    out[...] = (gate_val * sigma * up_val).astype(BF16)


def swiglu_grads(order, pre_ref, hidden_ref, *refs):
    gate_out, up_out = refs[-2:]
    ff = gate_out.shape[1]
    grad = hidden_ref[...].astype(F32)
    gate_val = pre_ref[:, :ff].astype(F32)
    up_val = pre_ref[:, ff:].astype(F32)
    sigma = 1.0 / (1.0 + jnp.exp(-gate_val))
    gate_out[...] = (
        grad * up_val * sigma * (1.0 + gate_val * (1.0 - sigma))
    ).astype(BF16)
    up_out[...] = (grad * gate_val * sigma).astype(BF16)


def in_token_order(body, count, order, pieces):
    rows, width = pieces[0][0].shape[0] // 4, pieces[0][0].shape[1] // 2
    shape = jax.ShapeDtypeStruct((16 * rows, width), BF16)
    outs = ()
    for i in (0, 2, 3, 1):
        piece = pieces[i]
        outs = pl.pallas_call(
            body,
            grid_spec=pltpu.PrefetchScalarGridSpec(
                num_scalar_prefetch=1,
                grid=(4,),
                in_specs=[
                    pl.BlockSpec((rows, value.shape[1]), lambda j, at: (j, 0))
                    for value in piece
                ]
                + [pl.BlockSpec(memory_space=pl.ANY)] * len(outs),
                out_specs=[
                    pl.BlockSpec((rows, width), lambda j, at, i=i: (at[4 * i + j], 0))
                ]
                * count,
            ),
            out_shape=[shape] * count,
            input_output_aliases=(
                {1 + len(piece) + j: j for j in range(count)} if outs else {}
            ),
            compiler_params=pltpu.CompilerParams(vmem_limit_bytes=32 * 1024 * 1024),
            cost_estimate=pl.CostEstimate(
                flops=48 * rows * width,
                bytes_accessed=40 * rows * width,
                transcendentals=8 * rows * width,
            ),
        )(order, *piece, *outs)
    return outs


def local(activations, grad_output, gate_pre, up_pre, w_gate, w_up, w_down):
    contract_rows = (((0,), (0,)), ((), ()))
    x, y, z, k = [lax.axis_index(name) for name in AXES]
    a0 = jnp.where(k == 0, x, y)
    b0 = jnp.where(k == 0, y, x)
    ff = gate_pre.shape[1]
    rows = gate_pre.shape[0]
    way = 1 - 2 * k

    def block_at(position):
        a = (a0 + position // 4) % 4
        b = (b0 + position % 4) % 4
        return jnp.where(k == 0, 4 * a + b, 4 * b + a)

    def blocks(steps, swapped):
        steps, swapped = jnp.array(steps), jnp.array(swapped)
        return 2 * ((z + steps * way + 8) % 8) + (k + swapped) % 2

    order = block_at(jnp.arange(16, dtype=jnp.int32))
    send_far = blocks((4, 0, -3, -3), (1, 1, 1, 0))
    keep_far = blocks((4, 0, 3, 3), (0, 0, 0, 1))
    send_near = blocks((-2, -2, -1, -1), (1, 0, 1, 0))
    keep_near = blocks((2, 2, 1, 1), (0, 1, 0, 1))

    grad_whole = lax.all_gather(grad_output, ("z", "core"), axis=0, tiled=True)

    pre = gather_rows(jnp.concatenate([gate_pre, up_pre], axis=1))
    (hidden,) = in_token_order(swiglu_hidden, 1, order, [(v,) for v in pre])
    hidden, acts, grad_whole = join(hidden, activations, grad_whole)
    acts_whole = lax.all_gather(acts, ("z", "core"), axis=0, tiled=True)

    shares = {}
    for step in (2, 1, 3):
        share = block_product(
            [(grad_whole, w_down)], order[4 * step : 4 * step + 4], BF16
        )
        shares[step] = along_a(share, step)
    total = block_product([(grad_whole, w_down)], order[:4], F32)
    grad_down = lax.dot_general(
        hidden, grad_whole, contract_rows, preferred_element_type=F32
    ).astype(BF16)
    grad_down, total, *got = join(grad_down, total, *shares.values())
    for share in got:
        total = total + share.astype(F32)
    grad_hidden = total[:rows]
    for step in (2, 1, 3):
        share = total[step * rows : (step + 1) * rows]
        grad_hidden = grad_hidden + along_b(share, step)
    grad_hidden = gather_rows(grad_hidden.astype(BF16))
    grad_gate_pre, grad_up_pre = in_token_order(
        swiglu_grads, 2, order, list(zip(pre, grad_hidden))
    )

    terms = [(grad_gate_pre, w_gate), (grad_up_pre, w_up)]
    far = other_core(block_product(terms, send_far, F32))
    far = block_product(terms, keep_far, F32) + far
    near = other_core(block_product(terms, send_near, F32))
    near = block_product(terms, keep_near, F32) + near
    got = round_z(far[:rows].astype(BF16))
    got, near, acts_whole = join(got, near, acts_whole)
    mine = jnp.concatenate(
        [far[2 * rows : 3 * rows] + got.astype(F32), far[3 * rows :]], axis=0
    )
    got = round_z(mine.astype(BF16))
    grad_gate = lax.dot_general(
        acts_whole, grad_gate_pre, contract_rows, preferred_element_type=F32
    ).astype(BF16)
    got, grad_gate = join(got, grad_gate)
    mine = near[: 2 * rows] + got.astype(F32)
    got = round_z(mine.astype(BF16))
    grad_up = lax.dot_general(
        acts_whole, grad_up_pre, contract_rows, preferred_element_type=F32
    ).astype(BF16)
    got, grad_up = join(got, grad_up)
    mine = near[2 * rows :] + got.astype(F32)
    got = round_z(mine.astype(BF16)).astype(F32)
    grad_input = far[rows : 2 * rows] + got[:rows] + other_core(got[rows:])
    return (grad_input.astype(BF16), grad_gate, grad_up, grad_down)


def solution(mesh):
    grid = Mesh(mesh.devices.reshape(DIMS), AXES)
    row, col = ("x", "y"), ("z", "core")
    in_specs = (
        P(col, row),
        P(col, row),
        P(row, col),
        P(row, col),
        P(row, col),
        P(row, col),
        P(col, row),
    )
    out_specs = (P(col, row), P(row, col), P(row, col), P(col, row))
    return jax.shard_map(
        local, mesh=grid, in_specs=in_specs, out_specs=out_specs, check_vma=False
    )
```

time: 425 us -> 189 us (0.44)
  waiting for transfers between devices: 360 us -> 53.9 us
  starting transfers between devices: 0.45 us -> 58.1 us
  Pallas kernels: 0 us -> 35.5 us
  matrix products: 40.5 us -> 12.4 us
  other arithmetic: 3.6 us -> 8.46 us
    all_gather x5 -> x2, waiting for transfers between devices: 214 us -> 2.28 us  [the longest x1 2.28 us: local(): grad_whole = lax.all_gather(grad_output, ('z', 'core'), axis=0, tiled=True)]
    reduce_scatter x2 -> x0, waiting for transfers between devices: 144 us -> none  [the longest x1 79.2 us: local(): lax.psum_scatter(lax.dot_general(grad_whole, w_down, contract_cols, prefe...]
    ppermute x0 -> x25, starting transfers between devices: none -> 58.1 us  [send(): return lax.ppermute(value, AXES, device_pairs(target))]
    ppermute x0 -> x25, waiting for transfers between devices: none -> 50.9 us  [send(): return lax.ppermute(value, AXES, device_pairs(target))]
    pallas_call x0 -> x16, Pallas kernels: none -> 35.5 us  [the longest x8 21.3 us: in_token_order(): pl.pallas_call(body, grid_spec=pltpu.PrefetchScalarGridSpec(num_scalar_pr...]
    dot_general x6 -> x3, matrix products: 40.5 us -> 12.4 us  [the longest x1 5.69 us: local(): lax.dot_general(acts_whole, grad_gate_pre, contract_rows, preferred_eleme...]
  transfers between devices with their start and end apart: 7 -> 27, of which waited for: 7 -> 17; matrix products, arithmetic and copies ran while one was open for 9% -> 10% of each run, Pallas kernels for 0% -> 19%
where the time goes in v1:
time: 189 us
  starting transfers between devices  58.1 us (31%)
  waiting for transfers between devices  53.9 us (29%)
  Pallas kernels  35.5 us (19%)
  between operations  14.4 us (8%)
  matrix products  12.4 us (7%)
  other arithmetic  8.46 us (4%)
  local copies, waits for them, and re-layouts  5.64 us (3%)
    ppermute x25, starting transfers between devices, send(): return lax.ppermute(value, AXES, device_pairs(target))  58.1 us
    ppermute x25, waiting for transfers between devices, send(): return lax.ppermute(value, AXES, device_pairs(target))  50.9 us
    pallas_call x8, Pallas kernels, in_token_order(): pl.pallas_call(body, grid_spec=pltpu.PrefetchScalarGridSpec(num_scalar_pr...  21.3 us
    pallas_call x8, Pallas kernels, block_product(): pl.pallas_call(pair_product, grid_spec=grid_spec, out_shape=jax.ShapeDtyp...  14.2 us
    dot_general x1, matrix products, local(): lax.dot_general(acts_whole, grad_gate_pre, contract_rows, preferred_eleme...  5.69 us
    unnamed x39, local copies, waits for them, and re-layouts  4.52 us
  transfers between devices with their start and end apart: 27, of which 17 were waited for; matrix products, arithmetic and copies ran while one was open for 10% of the time, Pallas kernels for 19%

profile of v1, /device:TPU:1, one launch (start us, length us, event | category | flops | bytes accessed | tf_op | source)
XLA Modules:
  0.0 188.6 jit_solution(13981306059386205948)
XLA Ops:
  11.9 2.5 %collective-permute-start.1 = (bf16[128,1024]{1,0:T(8,128)(2,1)S(1)}, bf16[128,1024]{1,0:T(8,128)(2,1)S(1)}, u32[]{:S(2)}, u32[]{:S(2)}) collective-permute-start(bf16[128,1024]{1,0:T(8,128)(2,1)S(1)} %constant_dynamic-update-slice_fusion), channel_id=1, source_target_pairs={{0,32},{1,129},{2,34},{3,131},{4,36},{5,133},{6,38},{7,135},{8,40}... | collective-permute-start | bytes 786440 | tf_op jit(solution)/shard_map/ppermute | solution.py:28
  16.9 4.3 %collective-permute-done.1 = bf16[128,1024]{1,0:T(8,128)(2,1)S(1)} collective-permute-done((bf16[128,1024]{1,0:T(8,128)(2,1)S(1)}, bf16[128,1024]{1,0:T(8,128)(2,1)S(1)}, u32[]{:S(2)}, u32[]{:S(2)}) %collective-permute-start.1) | collective-permute-done | bytes 262176 | tf_op jit(solution)/shard_map/ppermute | solution.py:28
  22.3 2.6 %collective-permute-start.5 = (bf16[512,1024]{1,0:T(8,128)(2,1)}, bf16[512,1024]{1,0:T(8,128)(2,1)}, u32[]{:S(2)}, u32[]{:S(2)}) collective-permute-start(bf16[512,1024]{1,0:T(8,128)(2,1)} %pad_maximum_fusion.pre_ref), channel_id=1, source_target_pairs={{0,128},{1,33},{2,130},{3,35},{4,132},{5,37},{6,134},{7,39},{8,136... | collective-permute-start | bytes 3145736 | tf_op jit(solution)/shard_map/ppermute | solution.py:28
  25.3 2.3 %collective-permute-start.3 = (bf16[512,1024]{1,0:T(8,128)(2,1)}, bf16[512,1024]{1,0:T(8,128)(2,1)}, u32[]{:S(2)}, u32[]{:S(2)}) collective-permute-start(bf16[512,1024]{1,0:T(8,128)(2,1)} %pad_maximum_fusion.pre_ref), channel_id=1, source_target_pairs={{0,192},{1,49},{2,194},{3,51},{4,196},{5,53},{6,198},{7,55},{8,200... | collective-permute-start | bytes 3145736 | tf_op jit(solution)/shard_map/ppermute | solution.py:28
  27.6 2.8 %shard_map.174.refs_0_ = bf16[2048,512]{1,0:T(8,128)(2,1)S(1)} custom-call(s32[16]{0:T(128)S(1)} %broadcast_select_fusion.order, bf16[512,1024]{1,0:T(8,128)(2,1)} %pad_maximum_fusion.pre_ref), custom_call_target="tpu_custom_call" | custom-call | flops 3145728 | bytes 2621440 | tf_op jit(solution)/shard_map/pallas_call | solution.py:141
  30.4 7.7 %collective-permute-done.5.pre_ref = bf16[512,1024]{1,0:T(8,128)(2,1)} collective-permute-done((bf16[512,1024]{1,0:T(8,128)(2,1)}, bf16[512,1024]{1,0:T(8,128)(2,1)}, u32[]{:S(2)}, u32[]{:S(2)}) %collective-permute-start.5) | collective-permute-done | bytes 1048608 | tf_op jit(solution)/shard_map/ppermute | solution.py:28
  38.1 2.8 %shard_map.175.refs_0_ = bf16[2048,512]{1,0:T(8,128)(2,1)S(1)} custom-call(s32[16]{0:T(128)S(1)} %broadcast_select_fusion.order, bf16[512,1024]{1,0:T(8,128)(2,1)} %collective-permute-done.5.pre_ref, bf16[2048,512]{1,0:T(8,128)(2,1)S(1)} %shard_map.174.refs_0_), custom_call_target="tpu_custom_call", output_to_operand_aliasing={{}: (2, {})} | custom-call | flops 3145728 | bytes 2621440 | tf_op jit(solution)/shard_map/pallas_call | solution.py:141
  40.9 8.3 %collective-permute-done.4.pre_ref = bf16[512,1024]{1,0:T(8,128)(2,1)S(1)} collective-permute-done((bf16[512,1024]{1,0:T(8,128)(2,1)}, bf16[512,1024]{1,0:T(8,128)(2,1)S(1)}, u32[]{:S(2)}, u32[]{:S(2)}) %collective-permute-start.4) | collective-permute-done | bytes 1048608 | tf_op jit(solution)/shard_map/ppermute | solution.py:28
  51.1 2.8 %shard_map.177 = bf16[2048,512]{1,0:T(8,128)(2,1)S(1)} custom-call(s32[16]{0:T(128)S(1)} %broadcast_select_fusion.order, bf16[512,1024]{1,0:T(8,128)(2,1)} %collective-permute-done.3.pre_ref, bf16[2048,512]{1,0:T(8,128)(2,1)S(1)} %shard_map.176.refs_0_), custom_call_target="tpu_custom_call", output_to_operand_aliasing={{}: (2, {})} | custom-call | flops 3145728 | bytes 2621440 | tf_op jit(solution)/shard_map/pallas_call | solution.py:141
  53.9 2.3 %all-gather.3.cloned.1.call-done.refs_0_.refs_1_ = bf16[2048,1024]{1,0:T(8,128)(2,1)} async-done(((bf16[128,1024]{1,0:T(8,128)(2,1)}), bf16[2048,1024]{1,0:T(8,128)(2,1)}) %all-gather.3.cloned.1.call-update) | async-done | bytes 4194320 | tf_op jit(solution)/shard_map/all_gather | solution.py:194
  56.3 2.2 %copy-done = bf16[2048,1024]{1,0:T(8,128)(2,1)S(1)} copy-done((bf16[2048,1024]{1,0:T(8,128)(2,1)S(1)}, bf16[2048,1024]{1,0:T(8,128)(2,1)}, u32[]{:S(2)}) %copy-start) | copy-done | bytes 4194328
  60.0 2.9 %collective-permute-start.6 = (bf16[512,512]{1,0:T(8,128)(2,1)S(1)}, bf16[512,512]{1,0:T(8,128)(2,1)S(1)}, u32[]{:S(2)}, u32[]{:S(2)}) collective-permute-start(bf16[512,512]{1,0:T(8,128)(2,1)S(1)} %shard_map.179), channel_id=1, source_target_pairs={{0,128},{1,33},{2,130},{3,35},{4,132},{5,37},{6,134},{7,39},{8,136... | collective-permute-start | bytes 1572872 | tf_op jit(solution)/shard_map/ppermute | solution.py:28
  70.3 3.4 %convolution_convert_fusion.2 = bf16[512,1024]{1,0:T(8,128)(2,1)} fusion(bf16[2048,512]{1,0:T(8,128)(2,1)S(1)} %shard_map.177, bf16[2048,1024]{1,0:T(8,128)(2,1)S(1)} %copy-done.1), kind=kOutput, calls=%fused_computation.2 | convolution fusion | flops 2148007936 | bytes 7340032 | tf_op jit(solution)/shard_map/dot_general | solution.py:208
  76.1 2.5 %collective-permute-start.11 = (f32[128,512]{1,0:T(8,128)S(1)}, f32[128,512]{1,0:T(8,128)S(1)}, u32[]{:S(2)}, u32[]{:S(2)}) collective-permute-start(f32[128,512]{1,0:T(8,128)S(1)} %get-tuple-element.55), channel_id=1, source_target_pairs={{0,48},{1,193},{2,50},{3,195},{4,52},{5,197},{6,54},{7,199},{8,56}... | collective-permute-start | bytes 786440 | tf_op jit(solution)/shard_map/ppermute | solution.py:28
  81.9 6.2 %collective-permute-done.10 = f32[128,512]{1,0:T(8,128)S(1)} collective-permute-done((f32[128,512]{1,0:T(8,128)S(1)}, f32[128,512]{1,0:T(8,128)S(1)}, u32[]{:S(2)}, u32[]{:S(2)}) %collective-permute-start.10) | collective-permute-done | bytes 262176 | tf_op jit(solution)/shard_map/ppermute | solution.py:28
  91.0 4.2 %collective-permute-done.14 = bf16[128,512]{1,0:T(8,128)(2,1)S(1)} collective-permute-done((bf16[128,512]{1,0:T(8,128)(2,1)S(1)}, bf16[128,512]{1,0:T(8,128)(2,1)S(1)}, u32[]{:S(2)}, u32[]{:S(2)}) %collective-permute-start.14) | collective-permute-done | bytes 131104 | tf_op jit(solution)/shard_map/ppermute | solution.py:28
  95.8 2.8 %collective-permute-start.17 = (bf16[512,512]{1,0:T(8,128)(2,1)S(1)}, bf16[512,512]{1,0:T(8,128)(2,1)}, u32[]{:S(2)}, u32[]{:S(2)}) collective-permute-start(bf16[512,512]{1,0:T(8,128)(2,1)S(1)} %pad_maximum_fusion.1.hidden_ref), channel_id=1, source_target_pairs={{0,128},{1,33},{2,130},{3,35},{4,132},{5,37},{6,134},{7,39},{8,136... | collective-permute-start | bytes 1572872 | tf_op jit(solution)/shard_map/ppermute | solution.py:28
  101.2 3.0 %shard_map.182 = (bf16[2048,512]{1,0:T(8,128)(2,1)S(1)}, bf16[2048,512]{1,0:T(8,128)(2,1)S(1)}) custom-call(s32[16]{0:T(128)S(1)} %broadcast_select_fusion.order, bf16[512,1024]{1,0:T(8,128)(2,1)} %pad_maximum_fusion.pre_ref, bf16[512,512]{1,0:T(8,128)(2,1)S(1)} %pad_maximum_fusion.1.hidden_ref), custom_call_target="tpu_custom_call" | custom-call | flops 3145728 | bytes 2621440 | tf_op jit(solution)/shard_map/pallas_call | solution.py:141
  105.8 3.1 %shard_map.183 = (bf16[2048,512]{1,0:T(8,128)(2,1)S(1)}, bf16[2048,512]{1,0:T(8,128)(2,1)S(1)}) custom-call(s32[16]{0:T(128)S(1)} %broadcast_select_fusion.order, bf16[512,1024]{1,0:T(8,128)(2,1)} %collective-permute-done.5.pre_ref, bf16[512,512]{1,0:T(8,128)(2,1)} %collective-permute-done.17.hidden_ref, ...), custom_call_target="tpu_custom_call", output_to_operand_aliasing={{0}: (3, {}), {1}: (4, {})} | custom-call | flops 3145728 | bytes 2621440 | tf_op jit(solution)/shard_map/pallas_call | solution.py:141
  108.9 2.5 %collective-permute-done.16.hidden_ref = bf16[512,512]{1,0:T(8,128)(2,1)} collective-permute-done((bf16[512,512]{1,0:T(8,128)(2,1)S(1)}, bf16[512,512]{1,0:T(8,128)(2,1)}, u32[]{:S(2)}, u32[]{:S(2)}) %collective-permute-start.16) | collective-permute-done | bytes 524320 | tf_op jit(solution)/shard_map/ppermute | solution.py:28
  111.4 2.9 %shard_map.184 = (bf16[2048,512]{1,0:T(8,128)(2,1)S(1)}, bf16[2048,512]{1,0:T(8,128)(2,1)S(1)}) custom-call(s32[16]{0:T(128)S(1)} %broadcast_select_fusion.order, bf16[512,1024]{1,0:T(8,128)(2,1)S(1)} %copy-done.8, bf16[512,512]{1,0:T(8,128)(2,1)} %collective-permute-done.16.hidden_ref, ...), custom_call_target="tpu_custom_call", output_to_operand_aliasing={{0}: (3, {}), {1}: (4, {})} | custom-call | flops 3145728 | bytes 2621440 | tf_op jit(solution)/shard_map/pallas_call | solution.py:141
  114.3 3.0 %shard_map.185 = (bf16[2048,512]{1,0:T(8,128)(2,1)S(1)}, bf16[2048,512]{1,0:T(8,128)(2,1)S(1)}) custom-call(s32[16]{0:T(128)S(1)} %broadcast_select_fusion.order, bf16[512,1024]{1,0:T(8,128)(2,1)} %collective-permute-done.3.pre_ref, bf16[512,512]{1,0:T(8,128)(2,1)S(1)} %collective-permute-done.15.hidden_ref, ...), custom_call_target="tpu_custom_call", output_to_operand_aliasing={{0}: (3, {}), {1}: (4, {})} | custom-call | flops 3145728 | bytes 2621440 | tf_op jit(solution)/shard_map/pallas_call | solution.py:141
  119.5 5.5 %collective-permute-start.18 = (f32[512,1024]{1,0:T(8,128)S(1)}, f32[512,1024]{1,0:T(8,128)S(1)}, u32[]{:S(2)}, u32[]{:S(2)}) collective-permute-start(f32[512,1024]{1,0:T(8,128)S(1)} %shard_map.187), channel_id=1, source_target_pairs={{0,1},{1,0},{2,3},{3,2},{4,5},{5,4},{6,7},{7,6},{8,9},{9,8},{10,11... | collective-permute-start | bytes 6291464 | tf_op jit(solution)/shard_map/ppermute | solution.py:28
  131.3 8.8 %collective-permute-start.19 = (bf16[128,1024]{1,0:T(8,128)(2,1)S(1)}, bf16[128,1024]{1,0:T(8,128)(2,1)S(1)}, u32[]{:S(2)}, u32[]{:S(2)}) collective-permute-start(bf16[128,1024]{1,0:T(8,128)(2,1)S(1)} %get-tuple-element.52), channel_id=1, source_target_pairs={{0,2},{1,15},{2,4},{3,1},{4,6},{5,3},{6,8},{7,5},{8,10},{9,7},{10,... | collective-permute-start | bytes 786440 | tf_op jit(solution)/shard_map/ppermute | solution.py:28
  145.0 2.9 %collective-permute-start.21 = (bf16[256,1024]{1,0:T(8,128)(2,1)S(1)}, bf16[256,1024]{1,0:T(8,128)(2,1)S(1)}, u32[]{:S(2)}, u32[]{:S(2)}) collective-permute-start(bf16[256,1024]{1,0:T(8,128)(2,1)S(1)} %pad_maximum_fusion.2), channel_id=1, source_target_pairs={{0,2},{1,15},{2,4},{3,1},{4,6},{5,3},{6,8},{7,5},{8,10},{9,7},{10,... | collective-permute-start | bytes 1572872 | tf_op jit(solution)/shard_map/ppermute | solution.py:28
  147.9 5.7 %convolution_convert_fusion.1 = bf16[1024,512]{1,0:T(8,128)(2,1)} fusion(bf16[2048,1024]{1,0:T(8,128)(2,1)} %all-gather.5.cloned.1.call-done, bf16[2048,512]{1,0:T(8,128)(2,1)S(1)} %get-tuple-element.39.refs_0_.refs_1_), kind=kOutput, calls=%fused_computation.1 | convolution fusion | flops 2148007936 | bytes 7340032 | tf_op jit(solution)/shard_map/dot_general | solution.py:234
  154.2 3.2 %collective-permute-start.22 = (bf16[256,1024]{1,0:T(8,128)(2,1)S(1)}, bf16[256,1024]{1,0:T(8,128)(2,1)S(1)}, u32[]{:S(2)}, u32[]{:S(2)}) collective-permute-start(bf16[256,1024]{1,0:T(8,128)(2,1)S(1)} %add_convert_fusion.1), channel_id=1, source_target_pairs={{0,2},{1,15},{2,4},{3,1},{4,6},{5,3},{6,8},{7,5},{8,10},{9,7},{10,... | collective-permute-start | bytes 1572872 | tf_op jit(solution)/shard_map/ppermute | solution.py:28
  157.4 3.3 %convolution_convert_fusion = bf16[1024,512]{1,0:T(8,128)(2,1)} fusion(bf16[2048,1024]{1,0:T(8,128)(2,1)S(1)} %copy-done.18, bf16[2048,512]{1,0:T(8,128)(2,1)S(1)} %copy-done.3), kind=kOutput, calls=%fused_computation | convolution fusion | flops 2148007936 | bytes 7340032 | tf_op jit(solution)/shard_map/dot_general | solution.py:240
  160.7 2.8 %collective-permute-done.22 = bf16[256,1024]{1,0:T(8,128)(2,1)S(1)} collective-permute-done((bf16[256,1024]{1,0:T(8,128)(2,1)S(1)}, bf16[256,1024]{1,0:T(8,128)(2,1)S(1)}, u32[]{:S(2)}, u32[]{:S(2)}) %collective-permute-start.22) | collective-permute-done | bytes 524320 | tf_op jit(solution)/shard_map/ppermute | solution.py:28
  163.7 3.2 %collective-permute-start.23 = (bf16[256,1024]{1,0:T(8,128)(2,1)S(1)}, bf16[256,1024]{1,0:T(8,128)(2,1)S(1)}, u32[]{:S(2)}, u32[]{:S(2)}) collective-permute-start(bf16[256,1024]{1,0:T(8,128)(2,1)S(1)} %add_convert_fusion), channel_id=1, source_target_pairs={{0,2},{1,15},{2,4},{3,1},{4,6},{5,3},{6,8},{7,5},{8,10},{9,7},{10,... | collective-permute-start | bytes 1572872 | tf_op jit(solution)/shard_map/ppermute | solution.py:28
  166.9 6.1 %collective-permute-done.23 = bf16[256,1024]{1,0:T(8,128)(2,1)S(1)} collective-permute-done((bf16[256,1024]{1,0:T(8,128)(2,1)S(1)}, bf16[256,1024]{1,0:T(8,128)(2,1)S(1)}, u32[]{:S(2)}, u32[]{:S(2)}) %collective-permute-start.23) | collective-permute-done | bytes 524320 | tf_op jit(solution)/shard_map/ppermute | solution.py:28
  173.0 5.3 %collective-permute-start.24 = (f32[128,1024]{1,0:T(8,128)S(1)}, f32[128,1024]{1,0:T(8,128)S(1)}, u32[]{:S(2)}, u32[]{:S(2)}) collective-permute-start(f32[128,1024]{1,0:T(8,128)S(1)} %slice.75), channel_id=1, source_target_pairs={{0,1},{1,0},{2,3},{3,2},{4,5},{5,4},{6,7},{7,6},{8,9},{9,8},{10,11... | collective-permute-start | bytes 1572872 | tf_op jit(solution)/shard_map/ppermute | solution.py:28
  (103 shorter events, 50.5 us)
Async XLA Ops:
  7.2 49.0 %all-gather.3.cloned.1.call-start = ((), (), s32[]{:S(2)}) async-start(), calls=%async_computation | async-start | bytes 4456448 | tf_op jit(solution)/shard_map/all_gather | solution.py:194
  7.9 135.9 %all-gather.5.cloned.1.call-start = ((), (), s32[]{:S(2)}) async-start(), calls=%async_computation.1 | async-start | bytes 4456448 | tf_op jit(solution)/shard_map/all_gather | solution.py:199
  9.8 7.1 %collective-permute-start.2 = (bf16[128,1024]{1,0:T(8,128)(2,1)S(1)}, bf16[128,1024]{1,0:T(8,128)(2,1)S(1)}, u32[]{:S(2)}, u32[]{:S(2)}) collective-permute-start(bf16[128,1024]{1,0:T(8,128)(2,1)S(1)} %constant_dynamic-update-slice_fusion), channel_id=1, source_target_pairs={{0,16},{1,65},{2,18},{3,67},{4,20},{5,69},{6,22},{7,71},{8,24},{9,... | collective-permute-start | bytes 786440 | tf_op jit(solution)/shard_map/ppermute | solution.py:28
  11.9 9.3 %collective-permute-start.1 = (bf16[128,1024]{1,0:T(8,128)(2,1)S(1)}, bf16[128,1024]{1,0:T(8,128)(2,1)S(1)}, u32[]{:S(2)}, u32[]{:S(2)}) collective-permute-start(bf16[128,1024]{1,0:T(8,128)(2,1)S(1)} %constant_dynamic-update-slice_fusion), channel_id=1, source_target_pairs={{0,32},{1,129},{2,34},{3,131},{4,36},{5,133},{6,38},{7,135},{8,40}... | collective-permute-start | bytes 786440 | tf_op jit(solution)/shard_map/ppermute | solution.py:28
  14.3 6.9 %collective-permute-start = (bf16[128,1024]{1,0:T(8,128)(2,1)S(1)}, bf16[128,1024]{1,0:T(8,128)(2,1)S(1)}, u32[]{:S(2)}, u32[]{:S(2)}) collective-permute-start(bf16[128,1024]{1,0:T(8,128)(2,1)S(1)} %constant_dynamic-update-slice_fusion), channel_id=1, source_target_pairs={{0,48},{1,193},{2,50},{3,195},{4,52},{5,197},{6,54},{7,199},{8,56}... | collective-permute-start | bytes 786440 | tf_op jit(solution)/shard_map/ppermute | solution.py:28
  22.3 15.8 %collective-permute-start.5 = (bf16[512,1024]{1,0:T(8,128)(2,1)}, bf16[512,1024]{1,0:T(8,128)(2,1)}, u32[]{:S(2)}, u32[]{:S(2)}) collective-permute-start(bf16[512,1024]{1,0:T(8,128)(2,1)} %pad_maximum_fusion.pre_ref), channel_id=1, source_target_pairs={{0,128},{1,33},{2,130},{3,35},{4,132},{5,37},{6,134},{7,39},{8,136... | collective-permute-start | bytes 3145736 | tf_op jit(solution)/shard_map/ppermute | solution.py:28
  24.9 24.3 %collective-permute-start.4 = (bf16[512,1024]{1,0:T(8,128)(2,1)}, bf16[512,1024]{1,0:T(8,128)(2,1)S(1)}, u32[]{:S(2)}, u32[]{:S(2)}) collective-permute-start(bf16[512,1024]{1,0:T(8,128)(2,1)} %pad_maximum_fusion.pre_ref), channel_id=1, source_target_pairs={{0,64},{1,17},{2,66},{3,19},{4,68},{5,21},{6,70},{7,23},{8,72},{9,... | collective-permute-start | bytes 3145736 | tf_op jit(solution)/shard_map/ppermute | solution.py:28
  25.3 25.8 %collective-permute-start.3 = (bf16[512,1024]{1,0:T(8,128)(2,1)}, bf16[512,1024]{1,0:T(8,128)(2,1)}, u32[]{:S(2)}, u32[]{:S(2)}) collective-permute-start(bf16[512,1024]{1,0:T(8,128)(2,1)} %pad_maximum_fusion.pre_ref), channel_id=1, source_target_pairs={{0,192},{1,49},{2,194},{3,51},{4,196},{5,53},{6,198},{7,55},{8,200... | collective-permute-start | bytes 3145736 | tf_op jit(solution)/shard_map/ppermute | solution.py:28
  60.0 13.7 %collective-permute-start.6 = (bf16[512,512]{1,0:T(8,128)(2,1)S(1)}, bf16[512,512]{1,0:T(8,128)(2,1)S(1)}, u32[]{:S(2)}, u32[]{:S(2)}) collective-permute-start(bf16[512,512]{1,0:T(8,128)(2,1)S(1)} %shard_map.179), channel_id=1, source_target_pairs={{0,128},{1,33},{2,130},{3,35},{4,132},{5,37},{6,134},{7,39},{8,136... | collective-permute-start | bytes 1572872 | tf_op jit(solution)/shard_map/ppermute | solution.py:28
  64.4 11.2 %collective-permute-start.7 = (bf16[512,512]{1,0:T(8,128)(2,1)S(1)}, bf16[512,512]{1,0:T(8,128)(2,1)S(1)}, u32[]{:S(2)}, u32[]{:S(2)}) collective-permute-start(bf16[512,512]{1,0:T(8,128)(2,1)S(1)} %shard_map.180), channel_id=1, source_target_pairs={{0,64},{1,17},{2,66},{3,19},{4,68},{5,21},{6,70},{7,23},{8,72},{9,... | collective-permute-start | bytes 1572872 | tf_op jit(solution)/shard_map/ppermute | solution.py:28
  66.6 9.1 %collective-permute-start.8 = (bf16[512,512]{1,0:T(8,128)(2,1)S(1)}, bf16[512,512]{1,0:T(8,128)(2,1)S(1)}, u32[]{:S(2)}, u32[]{:S(2)}) collective-permute-start(bf16[512,512]{1,0:T(8,128)(2,1)S(1)} %shard_map.181), channel_id=1, source_target_pairs={{0,192},{1,49},{2,194},{3,51},{4,196},{5,53},{6,198},{7,55},{8,200... | collective-permute-start | bytes 1572872 | tf_op jit(solution)/shard_map/ppermute | solution.py:28
  76.0 25.2 %copy-start.16 = (s32[4]{0:T(128)S(1)}, s32[4]{0:T(128)}, u32[]{:S(2)}) copy-start(s32[4]{0:T(128)} %constant.134.clone) | copy-start | bytes 52
  76.0 25.2 %copy-start.17 = (s32[4]{0:T(128)S(1)}, s32[4]{0:T(128)}, u32[]{:S(2)}) copy-start(s32[4]{0:T(128)} %constant.133.clone) | copy-start | bytes 52
  76.1 5.8 %collective-permute-start.11 = (f32[128,512]{1,0:T(8,128)S(1)}, f32[128,512]{1,0:T(8,128)S(1)}, u32[]{:S(2)}, u32[]{:S(2)}) collective-permute-start(f32[128,512]{1,0:T(8,128)S(1)} %get-tuple-element.55), channel_id=1, source_target_pairs={{0,48},{1,193},{2,50},{3,195},{4,52},{5,197},{6,54},{7,199},{8,56}... | collective-permute-start | bytes 786440 | tf_op jit(solution)/shard_map/ppermute | solution.py:28
  78.6 9.5 %collective-permute-start.10 = (f32[128,512]{1,0:T(8,128)S(1)}, f32[128,512]{1,0:T(8,128)S(1)}, u32[]{:S(2)}, u32[]{:S(2)}) collective-permute-start(f32[128,512]{1,0:T(8,128)S(1)} %get-tuple-element.56), channel_id=1, source_target_pairs={{0,16},{1,65},{2,18},{3,67},{4,20},{5,69},{6,22},{7,71},{8,24},{9,... | collective-permute-start | bytes 786440 | tf_op jit(solution)/shard_map/ppermute | solution.py:28
  78.6 9.5 %collective-permute-start.9 = (f32[128,512]{1,0:T(8,128)S(1)}, f32[128,512]{1,0:T(8,128)S(1)}, u32[]{:S(2)}, u32[]{:S(2)}) collective-permute-start(f32[128,512]{1,0:T(8,128)S(1)} %get-tuple-element.54), channel_id=1, source_target_pairs={{0,32},{1,129},{2,34},{3,131},{4,36},{5,133},{6,38},{7,135},{8,40}... | collective-permute-start | bytes 786440 | tf_op jit(solution)/shard_map/ppermute | solution.py:28
  88.2 6.9 %collective-permute-start.14 = (bf16[128,512]{1,0:T(8,128)(2,1)S(1)}, bf16[128,512]{1,0:T(8,128)(2,1)S(1)}, u32[]{:S(2)}, u32[]{:S(2)}) collective-permute-start(bf16[128,512]{1,0:T(8,128)(2,1)S(1)} %fusion.5), channel_id=1, source_target_pairs={{0,16},{1,65},{2,18},{3,67},{4,20},{5,69},{6,22},{7,71},{8,24},{9,... | collective-permute-start | bytes 393224 | tf_op jit(solution)/shard_map/ppermute | solution.py:28
  88.3 6.8 %collective-permute-start.13 = (bf16[128,512]{1,0:T(8,128)(2,1)S(1)}, bf16[128,512]{1,0:T(8,128)(2,1)S(1)}, u32[]{:S(2)}, u32[]{:S(2)}) collective-permute-start(bf16[128,512]{1,0:T(8,128)(2,1)S(1)} %fusion.5), channel_id=1, source_target_pairs={{0,32},{1,129},{2,34},{3,131},{4,36},{5,133},{6,38},{7,135},{8,40}... | collective-permute-start | bytes 393224 | tf_op jit(solution)/shard_map/ppermute | solution.py:28
  89.4 6.4 %collective-permute-start.12 = (bf16[128,512]{1,0:T(8,128)(2,1)S(1)}, bf16[128,512]{1,0:T(8,128)(2,1)S(1)}, u32[]{:S(2)}, u32[]{:S(2)}) collective-permute-start(bf16[128,512]{1,0:T(8,128)(2,1)S(1)} %fusion.5), channel_id=1, source_target_pairs={{0,48},{1,193},{2,50},{3,195},{4,52},{5,197},{6,54},{7,199},{8,56}... | collective-permute-start | bytes 393224 | tf_op jit(solution)/shard_map/ppermute | solution.py:28
  95.8 10.1 %collective-permute-start.17 = (bf16[512,512]{1,0:T(8,128)(2,1)S(1)}, bf16[512,512]{1,0:T(8,128)(2,1)}, u32[]{:S(2)}, u32[]{:S(2)}) collective-permute-start(bf16[512,512]{1,0:T(8,128)(2,1)S(1)} %pad_maximum_fusion.1.hidden_ref), channel_id=1, source_target_pairs={{0,128},{1,33},{2,130},{3,35},{4,132},{5,37},{6,134},{7,39},{8,136... | collective-permute-start | bytes 1572872 | tf_op jit(solution)/shard_map/ppermute | solution.py:28
  98.5 12.9 %collective-permute-start.16 = (bf16[512,512]{1,0:T(8,128)(2,1)S(1)}, bf16[512,512]{1,0:T(8,128)(2,1)}, u32[]{:S(2)}, u32[]{:S(2)}) collective-permute-start(bf16[512,512]{1,0:T(8,128)(2,1)S(1)} %pad_maximum_fusion.1.hidden_ref), channel_id=1, source_target_pairs={{0,64},{1,17},{2,66},{3,19},{4,68},{5,21},{6,70},{7,23},{8,72},{9,... | collective-permute-start | bytes 1572872 | tf_op jit(solution)/shard_map/ppermute | solution.py:28
  99.2 15.1 %collective-permute-start.15 = (bf16[512,512]{1,0:T(8,128)(2,1)S(1)}, bf16[512,512]{1,0:T(8,128)(2,1)S(1)}, u32[]{:S(2)}, u32[]{:S(2)}) collective-permute-start(bf16[512,512]{1,0:T(8,128)(2,1)S(1)} %pad_maximum_fusion.1.hidden_ref), channel_id=1, source_target_pairs={{0,192},{1,49},{2,194},{3,51},{4,196},{5,53},{6,198},{7,55},{8,200... | collective-permute-start | bytes 1572872 | tf_op jit(solution)/shard_map/ppermute | solution.py:28
  117.4 22.6 %copy-start.2 = (bf16[2048,512]{1,0:T(8,128)(2,1)}, bf16[2048,512]{1,0:T(8,128)(2,1)S(1)}, u32[]{:S(2)}) copy-start(bf16[2048,512]{1,0:T(8,128)(2,1)S(1)} %get-tuple-element.40.refs_3_.refs_4_) | copy-start | bytes 6291460
  119.5 9.9 %collective-permute-start.18 = (f32[512,1024]{1,0:T(8,128)S(1)}, f32[512,1024]{1,0:T(8,128)S(1)}, u32[]{:S(2)}, u32[]{:S(2)}) collective-permute-start(f32[512,1024]{1,0:T(8,128)S(1)} %shard_map.187), channel_id=1, source_target_pairs={{0,1},{1,0},{2,3},{3,2},{4,5},{5,4},{6,7},{7,6},{8,9},{9,8},{10,11... | collective-permute-start | bytes 6291464 | tf_op jit(solution)/shard_map/ppermute | solution.py:28
  127.1 14.9 %collective-permute-start.20 = (f32[512,1024]{1,0:T(8,128)S(1)}, f32[512,1024]{1,0:T(8,128)S(1)}, u32[]{:S(2)}, u32[]{:S(2)}) collective-permute-start(f32[512,1024]{1,0:T(8,128)S(1)} %shard_map.189), channel_id=1, source_target_pairs={{0,1},{1,0},{2,3},{3,2},{4,5},{5,4},{6,7},{7,6},{8,9},{9,8},{10,11... | collective-permute-start | bytes 6291464 | tf_op jit(solution)/shard_map/ppermute | solution.py:28
  131.3 12.5 %collective-permute-start.19 = (bf16[128,1024]{1,0:T(8,128)(2,1)S(1)}, bf16[128,1024]{1,0:T(8,128)(2,1)S(1)}, u32[]{:S(2)}, u32[]{:S(2)}) collective-permute-start(bf16[128,1024]{1,0:T(8,128)(2,1)S(1)} %get-tuple-element.52), channel_id=1, source_target_pairs={{0,2},{1,15},{2,4},{3,1},{4,6},{5,3},{6,8},{7,5},{8,10},{9,7},{10,... | collective-permute-start | bytes 786440 | tf_op jit(solution)/shard_map/ppermute | solution.py:28
  145.0 9.1 %copy-start.9 = (f32[512,1024]{1,0:T(8,128)S(1)}, f32[512,1024]{1,0:T(8,128)}, u32[]{:S(2)}) copy-start(f32[512,1024]{1,0:T(8,128)} %add.208) | copy-start | bytes 6291460
  145.0 9.1 %collective-permute-start.21 = (bf16[256,1024]{1,0:T(8,128)(2,1)S(1)}, bf16[256,1024]{1,0:T(8,128)(2,1)S(1)}, u32[]{:S(2)}, u32[]{:S(2)}) collective-permute-start(bf16[256,1024]{1,0:T(8,128)(2,1)S(1)} %pad_maximum_fusion.2), channel_id=1, source_target_pairs={{0,2},{1,15},{2,4},{3,1},{4,6},{5,3},{6,8},{7,5},{8,10},{9,7},{10,... | collective-permute-start | bytes 1572872 | tf_op jit(solution)/shard_map/ppermute | solution.py:28
  147.9 9.5 %copy-start.18 = (bf16[2048,1024]{1,0:T(8,128)(2,1)S(1)}, bf16[2048,1024]{1,0:T(8,128)(2,1)}, u32[]{:S(2)}) copy-start(bf16[2048,1024]{1,0:T(8,128)(2,1)} %all-gather.5.cloned.1.call-done) | copy-start | bytes 12582916
  154.2 9.3 %collective-permute-start.22 = (bf16[256,1024]{1,0:T(8,128)(2,1)S(1)}, bf16[256,1024]{1,0:T(8,128)(2,1)S(1)}, u32[]{:S(2)}, u32[]{:S(2)}) collective-permute-start(bf16[256,1024]{1,0:T(8,128)(2,1)S(1)} %add_convert_fusion.1), channel_id=1, source_target_pairs={{0,2},{1,15},{2,4},{3,1},{4,6},{5,3},{6,8},{7,5},{8,10},{9,7},{10,... | collective-permute-start | bytes 1572872 | tf_op jit(solution)/shard_map/ppermute | solution.py:28
  163.7 9.3 %collective-permute-start.23 = (bf16[256,1024]{1,0:T(8,128)(2,1)S(1)}, bf16[256,1024]{1,0:T(8,128)(2,1)S(1)}, u32[]{:S(2)}, u32[]{:S(2)}) collective-permute-start(bf16[256,1024]{1,0:T(8,128)(2,1)S(1)} %add_convert_fusion), channel_id=1, source_target_pairs={{0,2},{1,15},{2,4},{3,1},{4,6},{5,3},{6,8},{7,5},{8,10},{9,7},{10,... | collective-permute-start | bytes 1572872 | tf_op jit(solution)/shard_map/ppermute | solution.py:28
  173.0 6.9 %collective-permute-start.24 = (f32[128,1024]{1,0:T(8,128)S(1)}, f32[128,1024]{1,0:T(8,128)S(1)}, u32[]{:S(2)}, u32[]{:S(2)}) collective-permute-start(f32[128,1024]{1,0:T(8,128)S(1)} %slice.75), channel_id=1, source_target_pairs={{0,1},{1,0},{2,3},{3,2},{4,5},{5,4},{6,7},{7,6},{8,9},{9,8},{10,11... | collective-permute-start | bytes 1572872 | tf_op jit(solution)/shard_map/ppermute | solution.py:28
  (14 other events, 50.1 us)
Sparse Core Ops, SparseCore 0:
  9.8 46.3 all-gather.2
  58.0 42.6 all-gather.4

commit v2 on v1

--- a/solution.py
+++ b/solution.py
@@ -9,6 +9,7 @@
 DIMS = (4, 4, 8, 2)
 F32 = jnp.float32
 BF16 = jnp.bfloat16
+LIGHT = pl.CostEstimate(flops=1024, bytes_accessed=1024, transcendentals=0)
 
 
 def device_pairs(target):
@@ -78,7 +79,7 @@
     out[...] = total.astype(out.dtype)
 
 
-def block_product(terms, order, dtype):
+def block_product(terms, order, dtype, cost=None):
     n = order.shape[0]
     rows = terms[0][0].shape[0] // 16
     width, depth = terms[0][1].shape
@@ -101,7 +102,8 @@
         grid_spec=grid_spec,
         out_shape=jax.ShapeDtypeStruct((n * rows, width), dtype),
         compiler_params=pltpu.CompilerParams(vmem_limit_bytes=32 * 1024 * 1024),
-        cost_estimate=pl.CostEstimate(
+        cost_estimate=cost
+        or pl.CostEstimate(
             flops=2 * len(terms) * n * rows * width * depth,
             bytes_accessed=2 * len(terms) * (n * rows + width) * depth
             + n * rows * width * jnp.dtype(dtype).itemsize,
@@ -117,19 +119,6 @@
     up_val = pre_ref[:, ff:].astype(F32)
     sigma = 1.0 / (1.0 + jnp.exp(-gate_val))
     out[...] = (gate_val * sigma * up_val).astype(BF16)
-
-
-def swiglu_grads(order, pre_ref, hidden_ref, *refs):
-    gate_out, up_out = refs[-2:]
-    ff = gate_out.shape[1]
-    grad = hidden_ref[...].astype(F32)
-    gate_val = pre_ref[:, :ff].astype(F32)
-    up_val = pre_ref[:, ff:].astype(F32)
-    sigma = 1.0 / (1.0 + jnp.exp(-gate_val))
-    gate_out[...] = (
-        grad * up_val * sigma * (1.0 + gate_val * (1.0 - sigma))
-    ).astype(BF16)
-    up_out[...] = (grad * gate_val * sigma).astype(BF16)
 
 
 def in_token_order(body, count, order, pieces):
@@ -167,6 +156,72 @@
     return outs
 
 
+def swiglu_piece(hidden_ref, pre_ref, *refs):
+    gate_out, up_out = refs[-2:]
+    ff = gate_out.shape[1]
+    grad = hidden_ref[...].astype(F32)
+    gate_val = pre_ref[:, :ff].astype(F32)
+    up_val = pre_ref[:, ff:].astype(F32)
+    sigma = 1.0 / (1.0 + jnp.exp(-gate_val))
+    gate_out[...] = (
+        grad * up_val * sigma * (1.0 + gate_val * (1.0 - sigma))
+    ).astype(BF16)
+    up_out[...] = (grad * gate_val * sigma).astype(BF16)
+
+
+def swiglu_grads(grad_hidden, pre):
+    rows, ff = grad_hidden[0].shape
+    part = rows // 2
+    shape = jax.ShapeDtypeStruct((4 * rows, ff), BF16)
+    outs = ()
+    for i in (0, 2, 3, 1):
+        outs = pl.pallas_call(
+            swiglu_piece,
+            grid=(2,),
+            in_specs=[
+                pl.BlockSpec((part, ff), lambda j: (j, 0)),
+                pl.BlockSpec((part, 2 * ff), lambda j: (j, 0)),
+            ]
+            + [pl.BlockSpec(memory_space=pl.ANY)] * len(outs),
+            out_specs=[
+                pl.BlockSpec((part, ff), lambda j, i=i: (2 * i + j, 0)),
+                pl.BlockSpec((part, ff), lambda j, i=i: (2 * i + j, 0)),
+            ],
+            out_shape=[shape, shape],
+            input_output_aliases={2: 0, 3: 1} if outs else {},
+            compiler_params=pltpu.CompilerParams(vmem_limit_bytes=32 * 1024 * 1024),
+            cost_estimate=pl.CostEstimate(
+                flops=12 * rows * ff,
+                bytes_accessed=10 * rows * ff,
+                transcendentals=2 * rows * ff,
+            ),
+        )(grad_hidden[i], pre[i], *outs)
+    return outs
+
+
+def copy_blocks(order, *refs):
+    refs[-1][...] = jnp.concatenate([ref[...] for ref in refs[:-1]], axis=0)
+
+
+def reorder(value, order):
+    rows, width = value.shape[0] // 16, value.shape[1]
+    return pl.pallas_call(
+        copy_blocks,
+        grid_spec=pltpu.PrefetchScalarGridSpec(
+            num_scalar_prefetch=1,
+            grid=(4,),
+            in_specs=[
+                pl.BlockSpec((rows, width), lambda i, at, j=j: (at[4 * i + j], 0))
+                for j in range(4)
+            ],
+            out_specs=pl.BlockSpec((4 * rows, width), lambda i, at: (i, 0)),
+        ),
+        out_shape=jax.ShapeDtypeStruct(value.shape, value.dtype),
+        compiler_params=pltpu.CompilerParams(vmem_limit_bytes=32 * 1024 * 1024),
+        cost_estimate=LIGHT,
+    )(order, value, value, value, value)
+
+
 def local(activations, grad_output, gate_pre, up_pre, w_gate, w_up, w_down):
     contract_rows = (((0,), (0,)), ((), ()))
     x, y, z, k = [lax.axis_index(name) for name in AXES]
@@ -176,6 +231,12 @@
     rows = gate_pre.shape[0]
     way = 1 - 2 * k
 
+    def place(block):
+        up, along = block // 4, block % 4
+        a = jnp.where(k == 0, up, along)
+        b = jnp.where(k == 0, along, up)
+        return (a - a0) % 4 * 4 + (b - b0) % 4
+
     def block_at(position):
         a = (a0 + position // 4) % 4
         b = (b0 + position % 4) % 4
@@ -183,7 +244,7 @@
 
     def blocks(steps, swapped):
         steps, swapped = jnp.array(steps), jnp.array(swapped)
-        return 2 * ((z + steps * way + 8) % 8) + (k + swapped) % 2
+        return place(2 * ((z + steps * way + 8) % 8) + (k + swapped) % 2)
 
     order = block_at(jnp.arange(16, dtype=jnp.int32))
     send_far = blocks((4, 0, -3, -3), (1, 1, 1, 0))
@@ -216,33 +277,40 @@
         share = total[step * rows : (step + 1) * rows]
         grad_hidden = grad_hidden + along_b(share, step)
     grad_hidden = gather_rows(grad_hidden.astype(BF16))
-    grad_gate_pre, grad_up_pre = in_token_order(
-        swiglu_grads, 2, order, list(zip(pre, grad_hidden))
-    )
+    grad_gate_pre, grad_up_pre = swiglu_grads(grad_hidden, pre)
 
     terms = [(grad_gate_pre, w_gate), (grad_up_pre, w_up)]
-    far = other_core(block_product(terms, send_far, F32))
-    far = block_product(terms, keep_far, F32) + far
-    near = other_core(block_product(terms, send_near, F32))
-    near = block_product(terms, keep_near, F32) + near
-    got = round_z(far[:rows].astype(BF16))
+    far = other_core(block_product(terms, send_far, F32, LIGHT))
+    keep = block_product(terms, keep_far, F32, LIGHT)
+    first = (keep[:rows] + far[:rows]).astype(BF16)
+    gate_term, up_term, first, keep, far = join(
+        grad_gate_pre, grad_up_pre, first, keep, far
+    )
+    terms = [(gate_term, w_gate), (up_term, w_up)]
+    got = round_z(first)
+    near = other_core(block_product(terms, send_near, F32, LIGHT))
+    near = block_product(terms, keep_near, F32, LIGHT) + near
+    far = keep + far
     got, near, acts_whole = join(got, near, acts_whole)
     mine = jnp.concatenate(
         [far[2 * rows : 3 * rows] + got.astype(F32), far[3 * rows :]], axis=0
     )
     got = round_z(mine.astype(BF16))
+    acts_whole = reorder(acts_whole, order)
+    got, acts_whole = join(got, acts_whole)
+    mine = near[: 2 * rows] + got.astype(F32)
+    got = round_z(mine.astype(BF16))
     grad_gate = lax.dot_general(
-        acts_whole, grad_gate_pre, contract_rows, preferred_element_type=F32
+        acts_whole, gate_term, contract_rows, preferred_element_type=F32
     ).astype(BF16)
     got, grad_gate = join(got, grad_gate)
-    mine = near[: 2 * rows] + got.astype(F32)
+    mine = near[2 * rows :] + got.astype(F32)
     got = round_z(mine.astype(BF16))
     grad_up = lax.dot_general(
-        acts_whole, grad_up_pre, contract_rows, preferred_element_type=F32
+        acts_whole, up_term, contract_rows, preferred_element_type=F32
     ).astype(BF16)
     got, grad_up = join(got, grad_up)
-    mine = near[2 * rows :] + got.astype(F32)
-    got = round_z(mine.astype(BF16)).astype(F32)
+    got = got.astype(F32)
     grad_input = far[rows : 2 * rows] + got[:rows] + other_core(got[rows:])
     return (grad_input.astype(BF16), grad_gate, grad_up, grad_down)
 

time: 189 us -> 186 us (0.984)
  Pallas kernels: 35.5 us -> 31.5 us
  waiting for transfers between devices: 53.9 us -> 57.7 us
  matrix products: 12.4 us -> 10.1 us
  local copies, waits for them, and re-layouts: 5.64 us -> 7.82 us
    pallas_call x8 -> x4, Pallas kernels: 21.3 us -> 9.35 us  [in_token_order(): pl.pallas_call(body, grid_spec=pltpu.PrefetchScalarGridSpec(num_scalar_pr...]
    pallas_call x0 -> x5, Pallas kernels: none -> 7.92 us  [the longest x4 7.03 us: swiglu_grads(): pl.pallas_call(swiglu_piece, grid=(2,), in_specs=[pl.BlockSpec((part, ff)...]
    ppermute x25, waiting for transfers between devices: 50.9 us -> 54.7 us  [send(): return lax.ppermute(value, AXES, device_pairs(target))]
    dot_general x2, matrix products: 9.03 us -> 6.69 us  [the longest x1 3.36 us: local(): lax.dot_general(acts_whole, gate_term, contract_rows, preferred_element_t...]
    unnamed x39 -> x41, local copies, waits for them, and re-layouts: 4.52 us -> 6.71 us
  transfers between devices with their start and end apart: 27 -> 27, of which waited for: 17 -> 18; matrix products, arithmetic and copies ran while one was open for 10% -> 9% of each run, Pallas kernels for 19% -> 17%
where the time goes in v2:
time: 186 us
  waiting for transfers between devices  57.7 us (31%)
  starting transfers between devices  56.9 us (31%)
  Pallas kernels  31.5 us (17%)
  between operations  14.5 us (8%)
  matrix products  10.1 us (5%)
  local copies, waits for them, and re-layouts  7.82 us (4%)
  other arithmetic  7.47 us (4%)
    ppermute x25, starting transfers between devices, send(): return lax.ppermute(value, AXES, device_pairs(target))  56.8 us
    ppermute x25, waiting for transfers between devices, send(): return lax.ppermute(value, AXES, device_pairs(target))  54.7 us
    pallas_call x8, Pallas kernels, block_product(): pl.pallas_call(pair_product, grid_spec=grid_spec, out_shape=jax.ShapeDtyp...  14.2 us
    pallas_call x4, Pallas kernels, in_token_order(): pl.pallas_call(body, grid_spec=pltpu.PrefetchScalarGridSpec(num_scalar_pr...  9.35 us
    pallas_call x4, Pallas kernels, swiglu_grads(): pl.pallas_call(swiglu_piece, grid=(2,), in_specs=[pl.BlockSpec((part, ff)...  7.03 us
    unnamed x41, local copies, waits for them, and re-layouts  6.71 us
  transfers between devices with their start and end apart: 27, of which 18 were waited for; matrix products, arithmetic and copies ran while one was open for 9% of the time, Pallas kernels for 17%

profile of v2, /device:TPU:1, one launch (start us, length us, event | category | flops | bytes accessed | tf_op | source)
XLA Modules:
  0.0 185.9 jit_solution(8822716849200625354)
XLA Ops:
  9.8 2.1 %collective-permute-start.2 = (bf16[128,1024]{1,0:T(8,128)(2,1)S(1)}, bf16[128,1024]{1,0:T(8,128)(2,1)S(1)}, u32[]{:S(2)}, u32[]{:S(2)}) collective-permute-start(bf16[128,1024]{1,0:T(8,128)(2,1)S(1)} %constant_dynamic-update-slice_fusion), channel_id=1, source_target_pairs={{0,16},{1,65},{2,18},{3,67},{4,20},{5,69},{6,22},{7,71},{8,24},{9,... | collective-permute-start | bytes 786440 | tf_op jit(solution)/shard_map/ppermute | solution.py:29
  11.9 2.5 %collective-permute-start.1 = (bf16[128,1024]{1,0:T(8,128)(2,1)S(1)}, bf16[128,1024]{1,0:T(8,128)(2,1)S(1)}, u32[]{:S(2)}, u32[]{:S(2)}) collective-permute-start(bf16[128,1024]{1,0:T(8,128)(2,1)S(1)} %constant_dynamic-update-slice_fusion), channel_id=1, source_target_pairs={{0,32},{1,129},{2,34},{3,131},{4,36},{5,133},{6,38},{7,135},{8,40}... | collective-permute-start | bytes 786440 | tf_op jit(solution)/shard_map/ppermute | solution.py:29
  16.9 4.3 %collective-permute-done.1 = bf16[128,1024]{1,0:T(8,128)(2,1)S(1)} collective-permute-done((bf16[128,1024]{1,0:T(8,128)(2,1)S(1)}, bf16[128,1024]{1,0:T(8,128)(2,1)S(1)}, u32[]{:S(2)}, u32[]{:S(2)}) %collective-permute-start.1) | collective-permute-done | bytes 262176 | tf_op jit(solution)/shard_map/ppermute | solution.py:29
  22.3 2.6 %collective-permute-start.5 = (bf16[512,1024]{1,0:T(8,128)(2,1)}, bf16[512,1024]{1,0:T(8,128)(2,1)}, u32[]{:S(2)}, u32[]{:S(2)}) collective-permute-start(bf16[512,1024]{1,0:T(8,128)(2,1)} %pad_maximum_fusion.pre_ref), channel_id=1, source_target_pairs={{0,128},{1,33},{2,130},{3,35},{4,132},{5,37},{6,134},{7,39},{8,136... | collective-permute-start | bytes 3145736 | tf_op jit(solution)/shard_map/ppermute | solution.py:29
  25.3 2.3 %collective-permute-start.3 = (bf16[512,1024]{1,0:T(8,128)(2,1)}, bf16[512,1024]{1,0:T(8,128)(2,1)}, u32[]{:S(2)}, u32[]{:S(2)}) collective-permute-start(bf16[512,1024]{1,0:T(8,128)(2,1)} %pad_maximum_fusion.pre_ref), channel_id=1, source_target_pairs={{0,192},{1,49},{2,194},{3,51},{4,196},{5,53},{6,198},{7,55},{8,200... | collective-permute-start | bytes 3145736 | tf_op jit(solution)/shard_map/ppermute | solution.py:29
  27.6 2.8 %shard_map.174.refs_0_ = bf16[2048,512]{1,0:T(8,128)(2,1)S(1)} custom-call(s32[16]{0:T(128)S(1)} %broadcast_select_fusion.8.order, bf16[512,1024]{1,0:T(8,128)(2,1)} %pad_maximum_fusion.pre_ref), custom_call_target="tpu_custom_call" | custom-call | flops 3145728 | bytes 2621440 | tf_op jit(solution)/shard_map/pallas_call | solution.py:130
  30.4 7.7 %collective-permute-done.5.pre_ref = bf16[512,1024]{1,0:T(8,128)(2,1)} collective-permute-done((bf16[512,1024]{1,0:T(8,128)(2,1)}, bf16[512,1024]{1,0:T(8,128)(2,1)}, u32[]{:S(2)}, u32[]{:S(2)}) %collective-permute-start.5) | collective-permute-done | bytes 1048608 | tf_op jit(solution)/shard_map/ppermute | solution.py:29
  38.1 2.8 %shard_map.175.refs_0_ = bf16[2048,512]{1,0:T(8,128)(2,1)S(1)} custom-call(s32[16]{0:T(128)S(1)} %broadcast_select_fusion.8.order, bf16[512,1024]{1,0:T(8,128)(2,1)} %collective-permute-done.5.pre_ref, bf16[2048,512]{1,0:T(8,128)(2,1)S(1)} %shard_map.174.refs_0_), custom_call_target="tpu_custom_call", output_to_operand_aliasing={{}: (2, {})} | custom-call | flops 3145728 | bytes 2621440 | tf_op jit(solution)/shard_map/pallas_call | solution.py:130
  40.9 8.3 %collective-permute-done.4.pre_ref = bf16[512,1024]{1,0:T(8,128)(2,1)S(1)} collective-permute-done((bf16[512,1024]{1,0:T(8,128)(2,1)}, bf16[512,1024]{1,0:T(8,128)(2,1)S(1)}, u32[]{:S(2)}, u32[]{:S(2)}) %collective-permute-start.4) | collective-permute-done | bytes 1048608 | tf_op jit(solution)/shard_map/ppermute | solution.py:29
  51.1 2.8 %shard_map.177 = bf16[2048,512]{1,0:T(8,128)(2,1)S(1)} custom-call(s32[16]{0:T(128)S(1)} %broadcast_select_fusion.8.order, bf16[512,1024]{1,0:T(8,128)(2,1)} %collective-permute-done.3.pre_ref, bf16[2048,512]{1,0:T(8,128)(2,1)S(1)} %shard_map.176.refs_0_), custom_call_target="tpu_custom_call", output_to_operand_aliasing={{}: (2, {})} | custom-call | flops 3145728 | bytes 2621440 | tf_op jit(solution)/shard_map/pallas_call | solution.py:130
  53.9 2.3 %all-gather.3.cloned.1.call-done.refs_0_.refs_1_ = bf16[2048,1024]{1,0:T(8,128)(2,1)} async-done(((bf16[128,1024]{1,0:T(8,128)(2,1)}), bf16[2048,1024]{1,0:T(8,128)(2,1)}) %all-gather.3.cloned.1.call-update) | async-done | bytes 4194320 | tf_op jit(solution)/shard_map/all_gather | solution.py:255
  56.3 2.2 %copy-done = bf16[2048,1024]{1,0:T(8,128)(2,1)S(1)} copy-done((bf16[2048,1024]{1,0:T(8,128)(2,1)S(1)}, bf16[2048,1024]{1,0:T(8,128)(2,1)}, u32[]{:S(2)}) %copy-start) | copy-done | bytes 4194328
  60.0 2.9 %collective-permute-start.6 = (bf16[512,512]{1,0:T(8,128)(2,1)S(1)}, bf16[512,512]{1,0:T(8,128)(2,1)S(1)}, u32[]{:S(2)}, u32[]{:S(2)}) collective-permute-start(bf16[512,512]{1,0:T(8,128)(2,1)S(1)} %shard_map.179), channel_id=1, source_target_pairs={{0,128},{1,33},{2,130},{3,35},{4,132},{5,37},{6,134},{7,39},{8,136... | collective-permute-start | bytes 1572872 | tf_op jit(solution)/shard_map/ppermute | solution.py:29
  66.6 2.2 %collective-permute-start.8 = (bf16[512,512]{1,0:T(8,128)(2,1)S(1)}, bf16[512,512]{1,0:T(8,128)(2,1)S(1)}, u32[]{:S(2)}, u32[]{:S(2)}) collective-permute-start(bf16[512,512]{1,0:T(8,128)(2,1)S(1)} %shard_map.181), channel_id=1, source_target_pairs={{0,192},{1,49},{2,194},{3,51},{4,196},{5,53},{6,198},{7,55},{8,200... | collective-permute-start | bytes 1572872 | tf_op jit(solution)/shard_map/ppermute | solution.py:29
  70.3 3.4 %convolution_convert_fusion.2 = bf16[512,1024]{1,0:T(8,128)(2,1)} fusion(bf16[2048,512]{1,0:T(8,128)(2,1)S(1)} %shard_map.177, bf16[2048,1024]{1,0:T(8,128)(2,1)S(1)} %copy-done.1), kind=kOutput, calls=%fused_computation.2 | convolution fusion | flops 2148007936 | bytes 7340032 | tf_op jit(solution)/shard_map/dot_general | solution.py:269
  76.1 2.5 %collective-permute-start.11 = (f32[128,512]{1,0:T(8,128)S(1)}, f32[128,512]{1,0:T(8,128)S(1)}, u32[]{:S(2)}, u32[]{:S(2)}) collective-permute-start(f32[128,512]{1,0:T(8,128)S(1)} %get-tuple-element.65), channel_id=1, source_target_pairs={{0,48},{1,193},{2,50},{3,195},{4,52},{5,197},{6,54},{7,199},{8,56}... | collective-permute-start | bytes 786440 | tf_op jit(solution)/shard_map/ppermute | solution.py:29
  81.9 6.2 %collective-permute-done.10 = f32[128,512]{1,0:T(8,128)S(1)} collective-permute-done((f32[128,512]{1,0:T(8,128)S(1)}, f32[128,512]{1,0:T(8,128)S(1)}, u32[]{:S(2)}, u32[]{:S(2)}) %collective-permute-start.10) | collective-permute-done | bytes 262176 | tf_op jit(solution)/shard_map/ppermute | solution.py:29
  91.0 4.2 %collective-permute-done.14 = bf16[128,512]{1,0:T(8,128)(2,1)S(1)} collective-permute-done((bf16[128,512]{1,0:T(8,128)(2,1)S(1)}, bf16[128,512]{1,0:T(8,128)(2,1)S(1)}, u32[]{:S(2)}, u32[]{:S(2)}) %collective-permute-start.14) | collective-permute-done | bytes 131104 | tf_op jit(solution)/shard_map/ppermute | solution.py:29
  95.8 2.8 %collective-permute-start.17 = (bf16[512,512]{1,0:T(8,128)(2,1)S(1)}, bf16[512,512]{1,0:T(8,128)(2,1)}, u32[]{:S(2)}, u32[]{:S(2)}) collective-permute-start(bf16[512,512]{1,0:T(8,128)(2,1)S(1)} %pad_maximum_fusion.1.hidden_ref), channel_id=1, source_target_pairs={{0,128},{1,33},{2,130},{3,35},{4,132},{5,37},{6,134},{7,39},{8,136... | collective-permute-start | bytes 1572872 | tf_op jit(solution)/shard_map/ppermute | solution.py:29
  103.0 2.9 %collective-permute-done.17.hidden_ref = bf16[512,512]{1,0:T(8,128)(2,1)} collective-permute-done((bf16[512,512]{1,0:T(8,128)(2,1)S(1)}, bf16[512,512]{1,0:T(8,128)(2,1)}, u32[]{:S(2)}, u32[]{:S(2)}) %collective-permute-start.17) | collective-permute-done | bytes 524320 | tf_op jit(solution)/shard_map/ppermute | solution.py:29
  107.7 3.7 %collective-permute-done.16.hidden_ref = bf16[512,512]{1,0:T(8,128)(2,1)} collective-permute-done((bf16[512,512]{1,0:T(8,128)(2,1)S(1)}, bf16[512,512]{1,0:T(8,128)(2,1)}, u32[]{:S(2)}, u32[]{:S(2)}) %collective-permute-start.16) | collective-permute-done | bytes 524320 | tf_op jit(solution)/shard_map/ppermute | solution.py:29
  117.1 5.5 %collective-permute-start.18 = (f32[512,1024]{1,0:T(8,128)S(1)}, f32[512,1024]{1,0:T(8,128)S(1)}, u32[]{:S(2)}, u32[]{:S(2)}) collective-permute-start(f32[512,1024]{1,0:T(8,128)S(1)} %shard_map.187), channel_id=1, source_target_pairs={{0,1},{1,0},{2,3},{3,2},{4,5},{5,4},{6,7},{7,6},{8,9},{9,8},{10,11... | collective-permute-start | bytes 6291464 | tf_op jit(solution)/shard_map/ppermute | solution.py:29
  129.0 8.7 %collective-permute-start.19 = (bf16[128,1024]{1,0:T(8,128)(2,1)S(1)}, bf16[128,1024]{1,0:T(8,128)(2,1)S(1)}, u32[]{:S(2)}, u32[]{:S(2)}) collective-permute-start(bf16[128,1024]{1,0:T(8,128)(2,1)S(1)} %fusion.3), channel_id=1, source_target_pairs={{0,2},{1,15},{2,4},{3,1},{4,6},{5,3},{6,8},{7,5},{8,10},{9,7},{10,... | collective-permute-start | bytes 786440 | tf_op jit(solution)/shard_map/ppermute | solution.py:29
  145.3 2.2 %copy-done.4 = bf16[2048,1024]{1,0:T(8,128)(2,1)S(1)} copy-done((bf16[2048,1024]{1,0:T(8,128)(2,1)S(1)}, bf16[2048,1024]{1,0:T(8,128)(2,1)}, u32[]{:S(2)}) %copy-start.4) | copy-done | bytes 4194328
  148.4 3.4 %collective-permute-done.21 = bf16[256,1024]{1,0:T(8,128)(2,1)S(1)} collective-permute-done((bf16[256,1024]{1,0:T(8,128)(2,1)S(1)}, bf16[256,1024]{1,0:T(8,128)(2,1)S(1)}, u32[]{:S(2)}, u32[]{:S(2)}) %collective-permute-start.21) | collective-permute-done | bytes 524320 | tf_op jit(solution)/shard_map/ppermute | solution.py:29
  152.0 3.0 %collective-permute-start.22 = (bf16[256,1024]{1,0:T(8,128)(2,1)S(1)}, bf16[256,1024]{1,0:T(8,128)(2,1)S(1)}, u32[]{:S(2)}, u32[]{:S(2)}) collective-permute-start(bf16[256,1024]{1,0:T(8,128)(2,1)S(1)} %add_convert_fusion.1), channel_id=1, source_target_pairs={{0,2},{1,15},{2,4},{3,1},{4,6},{5,3},{6,8},{7,5},{8,10},{9,7},{10,... | collective-permute-start | bytes 1572872 | tf_op jit(solution)/shard_map/ppermute | solution.py:29
  155.0 3.4 %convolution_convert_fusion.1 = bf16[1024,512]{1,0:T(8,128)(2,1)} fusion(bf16[2048,1024]{1,0:T(8,128)(2,1)S(1)} %shard_map.190, bf16[2048,512]{1,0:T(8,128)(2,1)S(1)} %get-tuple-element.51.refs_0_.refs_1_), kind=kOutput, calls=%fused_computation.1 | convolution fusion | flops 2148007936 | bytes 7340032 | tf_op jit(solution)/shard_map/dot_general | solution.py:303
  158.4 2.8 %collective-permute-done.22 = bf16[256,1024]{1,0:T(8,128)(2,1)S(1)} collective-permute-done((bf16[256,1024]{1,0:T(8,128)(2,1)S(1)}, bf16[256,1024]{1,0:T(8,128)(2,1)S(1)}, u32[]{:S(2)}, u32[]{:S(2)}) %collective-permute-start.22) | collective-permute-done | bytes 524320 | tf_op jit(solution)/shard_map/ppermute | solution.py:29
  161.3 3.2 %collective-permute-start.23 = (bf16[256,1024]{1,0:T(8,128)(2,1)S(1)}, bf16[256,1024]{1,0:T(8,128)(2,1)S(1)}, u32[]{:S(2)}, u32[]{:S(2)}) collective-permute-start(bf16[256,1024]{1,0:T(8,128)(2,1)S(1)} %add_convert_fusion), channel_id=1, source_target_pairs={{0,2},{1,15},{2,4},{3,1},{4,6},{5,3},{6,8},{7,5},{8,10},{9,7},{10,... | collective-permute-start | bytes 1572872 | tf_op jit(solution)/shard_map/ppermute | solution.py:29
  164.5 3.3 %convolution_convert_fusion = bf16[1024,512]{1,0:T(8,128)(2,1)} fusion(bf16[2048,1024]{1,0:T(8,128)(2,1)S(1)} %shard_map.190, bf16[2048,512]{1,0:T(8,128)(2,1)S(1)} %copy-done.3), kind=kOutput, calls=%fused_computation | convolution fusion | flops 2148007936 | bytes 7340032 | tf_op jit(solution)/shard_map/dot_general | solution.py:309
  167.8 2.8 %collective-permute-done.23 = bf16[256,1024]{1,0:T(8,128)(2,1)S(1)} collective-permute-done((bf16[256,1024]{1,0:T(8,128)(2,1)S(1)}, bf16[256,1024]{1,0:T(8,128)(2,1)S(1)}, u32[]{:S(2)}, u32[]{:S(2)}) %collective-permute-start.23) | collective-permute-done | bytes 524320 | tf_op jit(solution)/shard_map/ppermute | solution.py:29
  170.7 5.0 %collective-permute-start.24 = (f32[128,1024]{1,0:T(8,128)S(1)}, f32[128,1024]{1,0:T(8,128)S(1)}, u32[]{:S(2)}, u32[]{:S(2)}) collective-permute-start(f32[128,1024]{1,0:T(8,128)S(1)} %slice.79), channel_id=1, source_target_pairs={{0,1},{1,0},{2,3},{3,2},{4,5},{5,4},{6,7},{7,6},{8,9},{9,8},{10,11... | collective-permute-start | bytes 1572872 | tf_op jit(solution)/shard_map/ppermute | solution.py:29
  (108 shorter events, 55.0 us)
Async XLA Ops:
  7.2 49.0 %all-gather.3.cloned.1.call-start = ((), (), s32[]{:S(2)}) async-start(), calls=%async_computation | async-start | bytes 4456448 | tf_op jit(solution)/shard_map/all_gather | solution.py:255
  7.9 134.4 %all-gather.5.cloned.1.call-start = ((), (), s32[]{:S(2)}) async-start(), calls=%async_computation.1 | async-start | bytes 4456448 | tf_op jit(solution)/shard_map/all_gather | solution.py:260
  9.8 7.1 %collective-permute-start.2 = (bf16[128,1024]{1,0:T(8,128)(2,1)S(1)}, bf16[128,1024]{1,0:T(8,128)(2,1)S(1)}, u32[]{:S(2)}, u32[]{:S(2)}) collective-permute-start(bf16[128,1024]{1,0:T(8,128)(2,1)S(1)} %constant_dynamic-update-slice_fusion), channel_id=1, source_target_pairs={{0,16},{1,65},{2,18},{3,67},{4,20},{5,69},{6,22},{7,71},{8,24},{9,... | collective-permute-start | bytes 786440 | tf_op jit(solution)/shard_map/ppermute | solution.py:29
  11.9 9.3 %collective-permute-start.1 = (bf16[128,1024]{1,0:T(8,128)(2,1)S(1)}, bf16[128,1024]{1,0:T(8,128)(2,1)S(1)}, u32[]{:S(2)}, u32[]{:S(2)}) collective-permute-start(bf16[128,1024]{1,0:T(8,128)(2,1)S(1)} %constant_dynamic-update-slice_fusion), channel_id=1, source_target_pairs={{0,32},{1,129},{2,34},{3,131},{4,36},{5,133},{6,38},{7,135},{8,40}... | collective-permute-start | bytes 786440 | tf_op jit(solution)/shard_map/ppermute | solution.py:29
  14.3 6.9 %collective-permute-start = (bf16[128,1024]{1,0:T(8,128)(2,1)S(1)}, bf16[128,1024]{1,0:T(8,128)(2,1)S(1)}, u32[]{:S(2)}, u32[]{:S(2)}) collective-permute-start(bf16[128,1024]{1,0:T(8,128)(2,1)S(1)} %constant_dynamic-update-slice_fusion), channel_id=1, source_target_pairs={{0,48},{1,193},{2,50},{3,195},{4,52},{5,197},{6,54},{7,199},{8,56}... | collective-permute-start | bytes 786440 | tf_op jit(solution)/shard_map/ppermute | solution.py:29
  22.3 15.8 %collective-permute-start.5 = (bf16[512,1024]{1,0:T(8,128)(2,1)}, bf16[512,1024]{1,0:T(8,128)(2,1)}, u32[]{:S(2)}, u32[]{:S(2)}) collective-permute-start(bf16[512,1024]{1,0:T(8,128)(2,1)} %pad_maximum_fusion.pre_ref), channel_id=1, source_target_pairs={{0,128},{1,33},{2,130},{3,35},{4,132},{5,37},{6,134},{7,39},{8,136... | collective-permute-start | bytes 3145736 | tf_op jit(solution)/shard_map/ppermute | solution.py:29
  24.9 24.3 %collective-permute-start.4 = (bf16[512,1024]{1,0:T(8,128)(2,1)}, bf16[512,1024]{1,0:T(8,128)(2,1)S(1)}, u32[]{:S(2)}, u32[]{:S(2)}) collective-permute-start(bf16[512,1024]{1,0:T(8,128)(2,1)} %pad_maximum_fusion.pre_ref), channel_id=1, source_target_pairs={{0,64},{1,17},{2,66},{3,19},{4,68},{5,21},{6,70},{7,23},{8,72},{9,... | collective-permute-start | bytes 3145736 | tf_op jit(solution)/shard_map/ppermute | solution.py:29
  25.3 25.8 %collective-permute-start.3 = (bf16[512,1024]{1,0:T(8,128)(2,1)}, bf16[512,1024]{1,0:T(8,128)(2,1)}, u32[]{:S(2)}, u32[]{:S(2)}) collective-permute-start(bf16[512,1024]{1,0:T(8,128)(2,1)} %pad_maximum_fusion.pre_ref), channel_id=1, source_target_pairs={{0,192},{1,49},{2,194},{3,51},{4,196},{5,53},{6,198},{7,55},{8,200... | collective-permute-start | bytes 3145736 | tf_op jit(solution)/shard_map/ppermute | solution.py:29
  60.0 13.7 %collective-permute-start.6 = (bf16[512,512]{1,0:T(8,128)(2,1)S(1)}, bf16[512,512]{1,0:T(8,128)(2,1)S(1)}, u32[]{:S(2)}, u32[]{:S(2)}) collective-permute-start(bf16[512,512]{1,0:T(8,128)(2,1)S(1)} %shard_map.179), channel_id=1, source_target_pairs={{0,128},{1,33},{2,130},{3,35},{4,132},{5,37},{6,134},{7,39},{8,136... | collective-permute-start | bytes 1572872 | tf_op jit(solution)/shard_map/ppermute | solution.py:29
  64.4 11.2 %collective-permute-start.7 = (bf16[512,512]{1,0:T(8,128)(2,1)S(1)}, bf16[512,512]{1,0:T(8,128)(2,1)S(1)}, u32[]{:S(2)}, u32[]{:S(2)}) collective-permute-start(bf16[512,512]{1,0:T(8,128)(2,1)S(1)} %shard_map.180), channel_id=1, source_target_pairs={{0,64},{1,17},{2,66},{3,19},{4,68},{5,21},{6,70},{7,23},{8,72},{9,... | collective-permute-start | bytes 1572872 | tf_op jit(solution)/shard_map/ppermute | solution.py:29
  66.6 9.1 %collective-permute-start.8 = (bf16[512,512]{1,0:T(8,128)(2,1)S(1)}, bf16[512,512]{1,0:T(8,128)(2,1)S(1)}, u32[]{:S(2)}, u32[]{:S(2)}) collective-permute-start(bf16[512,512]{1,0:T(8,128)(2,1)S(1)} %shard_map.181), channel_id=1, source_target_pairs={{0,192},{1,49},{2,194},{3,51},{4,196},{5,53},{6,198},{7,55},{8,200... | collective-permute-start | bytes 1572872 | tf_op jit(solution)/shard_map/ppermute | solution.py:29
  76.0 25.2 %copy-start.18 = (s32[4]{0:T(128)S(1)}, s32[4]{0:T(128)}, u32[]{:S(2)}) copy-start(s32[4]{0:T(128)} %constant.225.clone) | copy-start | bytes 52
  76.0 25.2 %copy-start.19 = (s32[4]{0:T(128)S(1)}, s32[4]{0:T(128)}, u32[]{:S(2)}) copy-start(s32[4]{0:T(128)} %constant.224.clone) | copy-start | bytes 52
  76.1 5.8 %collective-permute-start.11 = (f32[128,512]{1,0:T(8,128)S(1)}, f32[128,512]{1,0:T(8,128)S(1)}, u32[]{:S(2)}, u32[]{:S(2)}) collective-permute-start(f32[128,512]{1,0:T(8,128)S(1)} %get-tuple-element.65), channel_id=1, source_target_pairs={{0,48},{1,193},{2,50},{3,195},{4,52},{5,197},{6,54},{7,199},{8,56}... | collective-permute-start | bytes 786440 | tf_op jit(solution)/shard_map/ppermute | solution.py:29
  78.6 9.5 %collective-permute-start.10 = (f32[128,512]{1,0:T(8,128)S(1)}, f32[128,512]{1,0:T(8,128)S(1)}, u32[]{:S(2)}, u32[]{:S(2)}) collective-permute-start(f32[128,512]{1,0:T(8,128)S(1)} %get-tuple-element.66), channel_id=1, source_target_pairs={{0,16},{1,65},{2,18},{3,67},{4,20},{5,69},{6,22},{7,71},{8,24},{9,... | collective-permute-start | bytes 786440 | tf_op jit(solution)/shard_map/ppermute | solution.py:29
  78.6 9.5 %collective-permute-start.9 = (f32[128,512]{1,0:T(8,128)S(1)}, f32[128,512]{1,0:T(8,128)S(1)}, u32[]{:S(2)}, u32[]{:S(2)}) collective-permute-start(f32[128,512]{1,0:T(8,128)S(1)} %get-tuple-element.64), channel_id=1, source_target_pairs={{0,32},{1,129},{2,34},{3,131},{4,36},{5,133},{6,38},{7,135},{8,40}... | collective-permute-start | bytes 786440 | tf_op jit(solution)/shard_map/ppermute | solution.py:29
  88.2 6.9 %collective-permute-start.14 = (bf16[128,512]{1,0:T(8,128)(2,1)S(1)}, bf16[128,512]{1,0:T(8,128)(2,1)S(1)}, u32[]{:S(2)}, u32[]{:S(2)}) collective-permute-start(bf16[128,512]{1,0:T(8,128)(2,1)S(1)} %fusion.6), channel_id=1, source_target_pairs={{0,16},{1,65},{2,18},{3,67},{4,20},{5,69},{6,22},{7,71},{8,24},{9,... | collective-permute-start | bytes 393224 | tf_op jit(solution)/shard_map/ppermute | solution.py:29
  88.3 6.8 %collective-permute-start.13 = (bf16[128,512]{1,0:T(8,128)(2,1)S(1)}, bf16[128,512]{1,0:T(8,128)(2,1)S(1)}, u32[]{:S(2)}, u32[]{:S(2)}) collective-permute-start(bf16[128,512]{1,0:T(8,128)(2,1)S(1)} %fusion.6), channel_id=1, source_target_pairs={{0,32},{1,129},{2,34},{3,131},{4,36},{5,133},{6,38},{7,135},{8,40}... | collective-permute-start | bytes 393224 | tf_op jit(solution)/shard_map/ppermute | solution.py:29
  89.4 6.4 %collective-permute-start.12 = (bf16[128,512]{1,0:T(8,128)(2,1)S(1)}, bf16[128,512]{1,0:T(8,128)(2,1)S(1)}, u32[]{:S(2)}, u32[]{:S(2)}) collective-permute-start(bf16[128,512]{1,0:T(8,128)(2,1)S(1)} %fusion.6), channel_id=1, source_target_pairs={{0,48},{1,193},{2,50},{3,195},{4,52},{5,197},{6,54},{7,199},{8,56}... | collective-permute-start | bytes 393224 | tf_op jit(solution)/shard_map/ppermute | solution.py:29
  95.8 10.1 %collective-permute-start.17 = (bf16[512,512]{1,0:T(8,128)(2,1)S(1)}, bf16[512,512]{1,0:T(8,128)(2,1)}, u32[]{:S(2)}, u32[]{:S(2)}) collective-permute-start(bf16[512,512]{1,0:T(8,128)(2,1)S(1)} %pad_maximum_fusion.1.hidden_ref), channel_id=1, source_target_pairs={{0,128},{1,33},{2,130},{3,35},{4,132},{5,37},{6,134},{7,39},{8,136... | collective-permute-start | bytes 1572872 | tf_op jit(solution)/shard_map/ppermute | solution.py:29
  98.5 12.9 %collective-permute-start.16 = (bf16[512,512]{1,0:T(8,128)(2,1)S(1)}, bf16[512,512]{1,0:T(8,128)(2,1)}, u32[]{:S(2)}, u32[]{:S(2)}) collective-permute-start(bf16[512,512]{1,0:T(8,128)(2,1)S(1)} %pad_maximum_fusion.1.hidden_ref), channel_id=1, source_target_pairs={{0,64},{1,17},{2,66},{3,19},{4,68},{5,21},{6,70},{7,23},{8,72},{9,... | collective-permute-start | bytes 1572872 | tf_op jit(solution)/shard_map/ppermute | solution.py:29
  99.2 13.8 %collective-permute-start.15 = (bf16[512,512]{1,0:T(8,128)(2,1)S(1)}, bf16[512,512]{1,0:T(8,128)(2,1)S(1)}, u32[]{:S(2)}, u32[]{:S(2)}) collective-permute-start(bf16[512,512]{1,0:T(8,128)(2,1)S(1)} %pad_maximum_fusion.1.hidden_ref), channel_id=1, source_target_pairs={{0,192},{1,49},{2,194},{3,51},{4,196},{5,53},{6,198},{7,55},{8,200... | collective-permute-start | bytes 1572872 | tf_op jit(solution)/shard_map/ppermute | solution.py:29
  114.9 22.8 %copy-start.2 = (bf16[2048,512]{1,0:T(8,128)(2,1)}, bf16[2048,512]{1,0:T(8,128)(2,1)S(1)}, u32[]{:S(2)}) copy-start(bf16[2048,512]{1,0:T(8,128)(2,1)S(1)} %get-tuple-element.52.refs_3_.refs_4_) | copy-start | bytes 6291460
  117.1 9.3 %collective-permute-start.18 = (f32[512,1024]{1,0:T(8,128)S(1)}, f32[512,1024]{1,0:T(8,128)S(1)}, u32[]{:S(2)}, u32[]{:S(2)}) collective-permute-start(f32[512,1024]{1,0:T(8,128)S(1)} %shard_map.187), channel_id=1, source_target_pairs={{0,1},{1,0},{2,3},{3,2},{4,5},{5,4},{6,7},{7,6},{8,9},{9,8},{10,11... | collective-permute-start | bytes 6291464 | tf_op jit(solution)/shard_map/ppermute | solution.py:29
  126.4 11.2 %copy-start.12 = (s32[4]{0:T(128)S(1)}, s32[4]{0:T(128)}, u32[]{:S(2)}) copy-start(s32[4]{0:T(128)} %constant.231.clone) | copy-start | bytes 52
  126.4 11.2 %copy-start.13 = (s32[4]{0:T(128)S(1)}, s32[4]{0:T(128)}, u32[]{:S(2)}) copy-start(s32[4]{0:T(128)} %constant.230.clone) | copy-start | bytes 52
  128.5 11.8 %collective-permute-start.20 = (f32[512,1024]{1,0:T(8,128)S(1)}, f32[512,1024]{1,0:T(8,128)S(1)}, u32[]{:S(2)}, u32[]{:S(2)}) collective-permute-start(f32[512,1024]{1,0:T(8,128)S(1)} %shard_map.189), channel_id=1, source_target_pairs={{0,1},{1,0},{2,3},{3,2},{4,5},{5,4},{6,7},{7,6},{8,9},{9,8},{10,11... | collective-permute-start | bytes 6291464 | tf_op jit(solution)/shard_map/ppermute | solution.py:29
  129.0 13.3 %collective-permute-start.19 = (bf16[128,1024]{1,0:T(8,128)(2,1)S(1)}, bf16[128,1024]{1,0:T(8,128)(2,1)S(1)}, u32[]{:S(2)}, u32[]{:S(2)}) collective-permute-start(bf16[128,1024]{1,0:T(8,128)(2,1)S(1)} %fusion.3), channel_id=1, source_target_pairs={{0,2},{1,15},{2,4},{3,1},{4,6},{5,3},{6,8},{7,5},{8,10},{9,7},{10,... | collective-permute-start | bytes 786440 | tf_op jit(solution)/shard_map/ppermute | solution.py:29
  143.4 8.4 %collective-permute-start.21 = (bf16[256,1024]{1,0:T(8,128)(2,1)S(1)}, bf16[256,1024]{1,0:T(8,128)(2,1)S(1)}, u32[]{:S(2)}, u32[]{:S(2)}) collective-permute-start(bf16[256,1024]{1,0:T(8,128)(2,1)S(1)} %pad_maximum_fusion.2), channel_id=1, source_target_pairs={{0,2},{1,15},{2,4},{3,1},{4,6},{5,3},{6,8},{7,5},{8,10},{9,7},{10,... | collective-permute-start | bytes 1572872 | tf_op jit(solution)/shard_map/ppermute | solution.py:29
  152.0 9.2 %collective-permute-start.22 = (bf16[256,1024]{1,0:T(8,128)(2,1)S(1)}, bf16[256,1024]{1,0:T(8,128)(2,1)S(1)}, u32[]{:S(2)}, u32[]{:S(2)}) collective-permute-start(bf16[256,1024]{1,0:T(8,128)(2,1)S(1)} %add_convert_fusion.1), channel_id=1, source_target_pairs={{0,2},{1,15},{2,4},{3,1},{4,6},{5,3},{6,8},{7,5},{8,10},{9,7},{10,... | collective-permute-start | bytes 1572872 | tf_op jit(solution)/shard_map/ppermute | solution.py:29
  161.3 9.3 %collective-permute-start.23 = (bf16[256,1024]{1,0:T(8,128)(2,1)S(1)}, bf16[256,1024]{1,0:T(8,128)(2,1)S(1)}, u32[]{:S(2)}, u32[]{:S(2)}) collective-permute-start(bf16[256,1024]{1,0:T(8,128)(2,1)S(1)} %add_convert_fusion), channel_id=1, source_target_pairs={{0,2},{1,15},{2,4},{3,1},{4,6},{5,3},{6,8},{7,5},{8,10},{9,7},{10,... | collective-permute-start | bytes 1572872 | tf_op jit(solution)/shard_map/ppermute | solution.py:29
  170.7 6.5 %collective-permute-start.24 = (f32[128,1024]{1,0:T(8,128)S(1)}, f32[128,1024]{1,0:T(8,128)S(1)}, u32[]{:S(2)}, u32[]{:S(2)}) collective-permute-start(f32[128,1024]{1,0:T(8,128)S(1)} %slice.79), channel_id=1, source_target_pairs={{0,1},{1,0},{2,3},{3,2},{4,5},{5,4},{6,7},{7,6},{8,9},{9,8},{10,11... | collective-permute-start | bytes 1572872 | tf_op jit(solution)/shard_map/ppermute | solution.py:29
  (15 other events, 65.1 us)
Sparse Core Ops, SparseCore 0:
  9.8 46.3 all-gather.2
  58.0 42.6 all-gather.4

commit v3 on v2

--- a/solution.py
+++ b/solution.py
@@ -282,14 +282,15 @@
     terms = [(grad_gate_pre, w_gate), (grad_up_pre, w_up)]
     far = other_core(block_product(terms, send_far, F32, LIGHT))
     keep = block_product(terms, keep_far, F32, LIGHT)
+    near = block_product(terms, send_near, F32, LIGHT)
+    far, keep, near = join(far, keep, near)
     first = (keep[:rows] + far[:rows]).astype(BF16)
     gate_term, up_term, first, keep, far = join(
         grad_gate_pre, grad_up_pre, first, keep, far
     )
     terms = [(gate_term, w_gate), (up_term, w_up)]
     got = round_z(first)
-    near = other_core(block_product(terms, send_near, F32, LIGHT))
-    near = block_product(terms, keep_near, F32, LIGHT) + near
+    near = block_product(terms, keep_near, F32, LIGHT) + other_core(near)
     far = keep + far
     got, near, acts_whole = join(got, near, acts_whole)
     mine = jnp.concatenate(

time: 186 us -> 185 us (level)
  transfers between devices with their start and end apart: 27 -> 27, of which waited for: 18 -> 17; matrix products, arithmetic and copies ran while one was open for 9% -> 9% of each run, Pallas kernels for 17% -> 17%
where the time goes in v3:
time: 185 us; the launch traced here: 184 us
  starting transfers between devices  57 us (31%)
  waiting for transfers between devices  56 us (30%)
  Pallas kernels  31.5 us (17%)
  between operations  14.5 us (8%)
  matrix products  10.1 us (5%)
  local copies, waits for them, and re-layouts  7.82 us (4%)
  other arithmetic  7.42 us (4%)
    ppermute x25, starting transfers between devices, send(): return lax.ppermute(value, AXES, device_pairs(target))  56.9 us
    ppermute x25, waiting for transfers between devices, send(): return lax.ppermute(value, AXES, device_pairs(target))  53 us
    pallas_call x8, Pallas kernels, block_product(): pl.pallas_call(pair_product, grid_spec=grid_spec, out_shape=jax.ShapeDtyp...  14.2 us
    pallas_call x4, Pallas kernels, in_token_order(): pl.pallas_call(body, grid_spec=pltpu.PrefetchScalarGridSpec(num_scalar_pr...  9.35 us
    pallas_call x4, Pallas kernels, swiglu_grads(): pl.pallas_call(swiglu_piece, grid=(2,), in_specs=[pl.BlockSpec((part, ff)...  7.03 us
    unnamed x41, local copies, waits for them, and re-layouts  6.71 us
  transfers between devices with their start and end apart: 27, of which 17 were waited for; matrix products, arithmetic and copies ran while one was open for 9% of the time, Pallas kernels for 17%

profile of v3, /device:TPU:1, one launch (start us, length us, event | category | flops | bytes accessed | tf_op | source)
XLA Modules:
  0.0 184.3 jit_solution(1039567662171646325)
XLA Ops:
  9.8 2.1 %collective-permute-start.2 = (bf16[128,1024]{1,0:T(8,128)(2,1)S(1)}, bf16[128,1024]{1,0:T(8,128)(2,1)S(1)}, u32[]{:S(2)}, u32[]{:S(2)}) collective-permute-start(bf16[128,1024]{1,0:T(8,128)(2,1)S(1)} %constant_dynamic-update-slice_fusion), channel_id=1, source_target_pairs={{0,16},{1,65},{2,18},{3,67},{4,20},{5,69},{6,22},{7,71},{8,24},{9,... | collective-permute-start | bytes 786440 | tf_op jit(solution)/shard_map/ppermute | solution.py:29
  11.9 2.5 %collective-permute-start.1 = (bf16[128,1024]{1,0:T(8,128)(2,1)S(1)}, bf16[128,1024]{1,0:T(8,128)(2,1)S(1)}, u32[]{:S(2)}, u32[]{:S(2)}) collective-permute-start(bf16[128,1024]{1,0:T(8,128)(2,1)S(1)} %constant_dynamic-update-slice_fusion), channel_id=1, source_target_pairs={{0,32},{1,129},{2,34},{3,131},{4,36},{5,133},{6,38},{7,135},{8,40}... | collective-permute-start | bytes 786440 | tf_op jit(solution)/shard_map/ppermute | solution.py:29
  16.9 4.3 %collective-permute-done.1 = bf16[128,1024]{1,0:T(8,128)(2,1)S(1)} collective-permute-done((bf16[128,1024]{1,0:T(8,128)(2,1)S(1)}, bf16[128,1024]{1,0:T(8,128)(2,1)S(1)}, u32[]{:S(2)}, u32[]{:S(2)}) %collective-permute-start.1) | collective-permute-done | bytes 262176 | tf_op jit(solution)/shard_map/ppermute | solution.py:29
  22.3 2.6 %collective-permute-start.5 = (bf16[512,1024]{1,0:T(8,128)(2,1)}, bf16[512,1024]{1,0:T(8,128)(2,1)}, u32[]{:S(2)}, u32[]{:S(2)}) collective-permute-start(bf16[512,1024]{1,0:T(8,128)(2,1)} %pad_maximum_fusion.pre_ref), channel_id=1, source_target_pairs={{0,128},{1,33},{2,130},{3,35},{4,132},{5,37},{6,134},{7,39},{8,136... | collective-permute-start | bytes 3145736 | tf_op jit(solution)/shard_map/ppermute | solution.py:29
  25.3 2.3 %collective-permute-start.3 = (bf16[512,1024]{1,0:T(8,128)(2,1)}, bf16[512,1024]{1,0:T(8,128)(2,1)}, u32[]{:S(2)}, u32[]{:S(2)}) collective-permute-start(bf16[512,1024]{1,0:T(8,128)(2,1)} %pad_maximum_fusion.pre_ref), channel_id=1, source_target_pairs={{0,192},{1,49},{2,194},{3,51},{4,196},{5,53},{6,198},{7,55},{8,200... | collective-permute-start | bytes 3145736 | tf_op jit(solution)/shard_map/ppermute | solution.py:29
  27.6 2.8 %shard_map.174.refs_0_ = bf16[2048,512]{1,0:T(8,128)(2,1)S(1)} custom-call(s32[16]{0:T(128)S(1)} %broadcast_select_fusion.8.order, bf16[512,1024]{1,0:T(8,128)(2,1)} %pad_maximum_fusion.pre_ref), custom_call_target="tpu_custom_call" | custom-call | flops 3145728 | bytes 2621440 | tf_op jit(solution)/shard_map/pallas_call | solution.py:130
  30.4 7.7 %collective-permute-done.5.pre_ref = bf16[512,1024]{1,0:T(8,128)(2,1)} collective-permute-done((bf16[512,1024]{1,0:T(8,128)(2,1)}, bf16[512,1024]{1,0:T(8,128)(2,1)}, u32[]{:S(2)}, u32[]{:S(2)}) %collective-permute-start.5) | collective-permute-done | bytes 1048608 | tf_op jit(solution)/shard_map/ppermute | solution.py:29
  38.1 2.8 %shard_map.175.refs_0_ = bf16[2048,512]{1,0:T(8,128)(2,1)S(1)} custom-call(s32[16]{0:T(128)S(1)} %broadcast_select_fusion.8.order, bf16[512,1024]{1,0:T(8,128)(2,1)} %collective-permute-done.5.pre_ref, bf16[2048,512]{1,0:T(8,128)(2,1)S(1)} %shard_map.174.refs_0_), custom_call_target="tpu_custom_call", output_to_operand_aliasing={{}: (2, {})} | custom-call | flops 3145728 | bytes 2621440 | tf_op jit(solution)/shard_map/pallas_call | solution.py:130
  40.9 8.3 %collective-permute-done.4.pre_ref = bf16[512,1024]{1,0:T(8,128)(2,1)S(1)} collective-permute-done((bf16[512,1024]{1,0:T(8,128)(2,1)}, bf16[512,1024]{1,0:T(8,128)(2,1)S(1)}, u32[]{:S(2)}, u32[]{:S(2)}) %collective-permute-start.4) | collective-permute-done | bytes 1048608 | tf_op jit(solution)/shard_map/ppermute | solution.py:29
  51.1 2.8 %shard_map.177 = bf16[2048,512]{1,0:T(8,128)(2,1)S(1)} custom-call(s32[16]{0:T(128)S(1)} %broadcast_select_fusion.8.order, bf16[512,1024]{1,0:T(8,128)(2,1)} %collective-permute-done.3.pre_ref, bf16[2048,512]{1,0:T(8,128)(2,1)S(1)} %shard_map.176.refs_0_), custom_call_target="tpu_custom_call", output_to_operand_aliasing={{}: (2, {})} | custom-call | flops 3145728 | bytes 2621440 | tf_op jit(solution)/shard_map/pallas_call | solution.py:130
  53.9 2.3 %all-gather.3.cloned.1.call-done.refs_0_.refs_1_ = bf16[2048,1024]{1,0:T(8,128)(2,1)} async-done(((bf16[128,1024]{1,0:T(8,128)(2,1)}), bf16[2048,1024]{1,0:T(8,128)(2,1)}) %all-gather.3.cloned.1.call-update) | async-done | bytes 4194320 | tf_op jit(solution)/shard_map/all_gather | solution.py:255
  56.3 2.2 %copy-done = bf16[2048,1024]{1,0:T(8,128)(2,1)S(1)} copy-done((bf16[2048,1024]{1,0:T(8,128)(2,1)S(1)}, bf16[2048,1024]{1,0:T(8,128)(2,1)}, u32[]{:S(2)}) %copy-start) | copy-done | bytes 4194328
  60.0 2.9 %collective-permute-start.6 = (bf16[512,512]{1,0:T(8,128)(2,1)S(1)}, bf16[512,512]{1,0:T(8,128)(2,1)S(1)}, u32[]{:S(2)}, u32[]{:S(2)}) collective-permute-start(bf16[512,512]{1,0:T(8,128)(2,1)S(1)} %shard_map.179), channel_id=1, source_target_pairs={{0,128},{1,33},{2,130},{3,35},{4,132},{5,37},{6,134},{7,39},{8,136... | collective-permute-start | bytes 1572872 | tf_op jit(solution)/shard_map/ppermute | solution.py:29
  66.6 2.2 %collective-permute-start.8 = (bf16[512,512]{1,0:T(8,128)(2,1)S(1)}, bf16[512,512]{1,0:T(8,128)(2,1)S(1)}, u32[]{:S(2)}, u32[]{:S(2)}) collective-permute-start(bf16[512,512]{1,0:T(8,128)(2,1)S(1)} %shard_map.181), channel_id=1, source_target_pairs={{0,192},{1,49},{2,194},{3,51},{4,196},{5,53},{6,198},{7,55},{8,200... | collective-permute-start | bytes 1572872 | tf_op jit(solution)/shard_map/ppermute | solution.py:29
  70.3 3.4 %convolution_convert_fusion.2 = bf16[512,1024]{1,0:T(8,128)(2,1)} fusion(bf16[2048,512]{1,0:T(8,128)(2,1)S(1)} %shard_map.177, bf16[2048,1024]{1,0:T(8,128)(2,1)S(1)} %copy-done.1), kind=kOutput, calls=%fused_computation.2 | convolution fusion | flops 2148007936 | bytes 7340032 | tf_op jit(solution)/shard_map/dot_general | solution.py:269
  76.1 2.5 %collective-permute-start.11 = (f32[128,512]{1,0:T(8,128)S(1)}, f32[128,512]{1,0:T(8,128)S(1)}, u32[]{:S(2)}, u32[]{:S(2)}) collective-permute-start(f32[128,512]{1,0:T(8,128)S(1)} %get-tuple-element.71), channel_id=1, source_target_pairs={{0,48},{1,193},{2,50},{3,195},{4,52},{5,197},{6,54},{7,199},{8,56}... | collective-permute-start | bytes 786440 | tf_op jit(solution)/shard_map/ppermute | solution.py:29
  81.9 6.2 %collective-permute-done.10 = f32[128,512]{1,0:T(8,128)S(1)} collective-permute-done((f32[128,512]{1,0:T(8,128)S(1)}, f32[128,512]{1,0:T(8,128)S(1)}, u32[]{:S(2)}, u32[]{:S(2)}) %collective-permute-start.10) | collective-permute-done | bytes 262176 | tf_op jit(solution)/shard_map/ppermute | solution.py:29
  91.0 4.2 %collective-permute-done.14 = bf16[128,512]{1,0:T(8,128)(2,1)S(1)} collective-permute-done((bf16[128,512]{1,0:T(8,128)(2,1)S(1)}, bf16[128,512]{1,0:T(8,128)(2,1)S(1)}, u32[]{:S(2)}, u32[]{:S(2)}) %collective-permute-start.14) | collective-permute-done | bytes 131104 | tf_op jit(solution)/shard_map/ppermute | solution.py:29
  95.8 2.8 %collective-permute-start.17 = (bf16[512,512]{1,0:T(8,128)(2,1)S(1)}, bf16[512,512]{1,0:T(8,128)(2,1)}, u32[]{:S(2)}, u32[]{:S(2)}) collective-permute-start(bf16[512,512]{1,0:T(8,128)(2,1)S(1)} %pad_maximum_fusion.1.hidden_ref), channel_id=1, source_target_pairs={{0,128},{1,33},{2,130},{3,35},{4,132},{5,37},{6,134},{7,39},{8,136... | collective-permute-start | bytes 1572872 | tf_op jit(solution)/shard_map/ppermute | solution.py:29
  103.0 2.9 %collective-permute-done.17.hidden_ref = bf16[512,512]{1,0:T(8,128)(2,1)} collective-permute-done((bf16[512,512]{1,0:T(8,128)(2,1)S(1)}, bf16[512,512]{1,0:T(8,128)(2,1)}, u32[]{:S(2)}, u32[]{:S(2)}) %collective-permute-start.17) | collective-permute-done | bytes 524320 | tf_op jit(solution)/shard_map/ppermute | solution.py:29
  107.7 3.7 %collective-permute-done.16.hidden_ref = bf16[512,512]{1,0:T(8,128)(2,1)} collective-permute-done((bf16[512,512]{1,0:T(8,128)(2,1)S(1)}, bf16[512,512]{1,0:T(8,128)(2,1)}, u32[]{:S(2)}, u32[]{:S(2)}) %collective-permute-start.16) | collective-permute-done | bytes 524320 | tf_op jit(solution)/shard_map/ppermute | solution.py:29
  117.1 5.5 %collective-permute-start.18 = (f32[512,1024]{1,0:T(8,128)S(1)}, f32[512,1024]{1,0:T(8,128)S(1)}, u32[]{:S(2)}, u32[]{:S(2)}) collective-permute-start(f32[512,1024]{1,0:T(8,128)S(1)} %shard_map.186), channel_id=1, source_target_pairs={{0,1},{1,0},{2,3},{3,2},{4,5},{5,4},{6,7},{7,6},{8,9},{9,8},{10,11... | collective-permute-start | bytes 6291464 | tf_op jit(solution)/shard_map/ppermute | solution.py:29
  127.0 8.8 %collective-permute-start.19 = (bf16[128,1024]{1,0:T(8,128)(2,1)S(1)}, bf16[128,1024]{1,0:T(8,128)(2,1)S(1)}, u32[]{:S(2)}, u32[]{:S(2)}) collective-permute-start(bf16[128,1024]{1,0:T(8,128)(2,1)S(1)} %add_convert_fusion.2), channel_id=1, source_target_pairs={{0,2},{1,15},{2,4},{3,1},{4,6},{5,3},{6,8},{7,5},{8,10},{9,7},{10,... | collective-permute-start | bytes 786440 | tf_op jit(solution)/shard_map/ppermute | solution.py:29
  143.4 2.2 %copy-done.4 = bf16[2048,1024]{1,0:T(8,128)(2,1)S(1)} copy-done((bf16[2048,1024]{1,0:T(8,128)(2,1)S(1)}, bf16[2048,1024]{1,0:T(8,128)(2,1)}, u32[]{:S(2)}) %copy-start.4) | copy-done | bytes 4194328
  146.5 3.4 %collective-permute-done.21 = bf16[256,1024]{1,0:T(8,128)(2,1)S(1)} collective-permute-done((bf16[256,1024]{1,0:T(8,128)(2,1)S(1)}, bf16[256,1024]{1,0:T(8,128)(2,1)S(1)}, u32[]{:S(2)}, u32[]{:S(2)}) %collective-permute-start.21) | collective-permute-done | bytes 524320 | tf_op jit(solution)/shard_map/ppermute | solution.py:29
  150.0 3.1 %collective-permute-start.22 = (bf16[256,1024]{1,0:T(8,128)(2,1)S(1)}, bf16[256,1024]{1,0:T(8,128)(2,1)S(1)}, u32[]{:S(2)}, u32[]{:S(2)}) collective-permute-start(bf16[256,1024]{1,0:T(8,128)(2,1)S(1)} %add_convert_fusion.1), channel_id=1, source_target_pairs={{0,2},{1,15},{2,4},{3,1},{4,6},{5,3},{6,8},{7,5},{8,10},{9,7},{10,... | collective-permute-start | bytes 1572872 | tf_op jit(solution)/shard_map/ppermute | solution.py:29
  153.1 3.4 %convolution_convert_fusion.1 = bf16[1024,512]{1,0:T(8,128)(2,1)} fusion(bf16[2048,1024]{1,0:T(8,128)(2,1)S(1)} %shard_map.190, bf16[2048,512]{1,0:T(8,128)(2,1)S(1)} %get-tuple-element.56.refs_0_.refs_1_), kind=kOutput, calls=%fused_computation.1 | convolution fusion | flops 2148007936 | bytes 7340032 | tf_op jit(solution)/shard_map/dot_general | solution.py:304
  156.4 2.8 %collective-permute-done.22 = bf16[256,1024]{1,0:T(8,128)(2,1)S(1)} collective-permute-done((bf16[256,1024]{1,0:T(8,128)(2,1)S(1)}, bf16[256,1024]{1,0:T(8,128)(2,1)S(1)}, u32[]{:S(2)}, u32[]{:S(2)}) %collective-permute-start.22) | collective-permute-done | bytes 524320 | tf_op jit(solution)/shard_map/ppermute | solution.py:29
  159.4 3.2 %collective-permute-start.23 = (bf16[256,1024]{1,0:T(8,128)(2,1)S(1)}, bf16[256,1024]{1,0:T(8,128)(2,1)S(1)}, u32[]{:S(2)}, u32[]{:S(2)}) collective-permute-start(bf16[256,1024]{1,0:T(8,128)(2,1)S(1)} %add_convert_fusion), channel_id=1, source_target_pairs={{0,2},{1,15},{2,4},{3,1},{4,6},{5,3},{6,8},{7,5},{8,10},{9,7},{10,... | collective-permute-start | bytes 1572872 | tf_op jit(solution)/shard_map/ppermute | solution.py:29
  162.6 3.3 %convolution_convert_fusion = bf16[1024,512]{1,0:T(8,128)(2,1)} fusion(bf16[2048,1024]{1,0:T(8,128)(2,1)S(1)} %shard_map.190, bf16[2048,512]{1,0:T(8,128)(2,1)S(1)} %copy-done.3), kind=kOutput, calls=%fused_computation | convolution fusion | flops 2148007936 | bytes 7340032 | tf_op jit(solution)/shard_map/dot_general | solution.py:310
  165.9 2.8 %collective-permute-done.23 = bf16[256,1024]{1,0:T(8,128)(2,1)S(1)} collective-permute-done((bf16[256,1024]{1,0:T(8,128)(2,1)S(1)}, bf16[256,1024]{1,0:T(8,128)(2,1)S(1)}, u32[]{:S(2)}, u32[]{:S(2)}) %collective-permute-start.23) | collective-permute-done | bytes 524320 | tf_op jit(solution)/shard_map/ppermute | solution.py:29
  168.7 5.3 %collective-permute-start.24 = (f32[128,1024]{1,0:T(8,128)S(1)}, f32[128,1024]{1,0:T(8,128)S(1)}, u32[]{:S(2)}, u32[]{:S(2)}) collective-permute-start(f32[128,1024]{1,0:T(8,128)S(1)} %slice.77), channel_id=1, source_target_pairs={{0,1},{1,0},{2,3},{3,2},{4,5},{5,4},{6,7},{7,6},{8,9},{9,8},{10,11... | collective-permute-start | bytes 1572872 | tf_op jit(solution)/shard_map/ppermute | solution.py:29
  (107 shorter events, 53.0 us)
Async XLA Ops:
  7.2 49.0 %all-gather.3.cloned.1.call-start = ((), (), s32[]{:S(2)}) async-start(), calls=%async_computation | async-start | bytes 4456448 | tf_op jit(solution)/shard_map/all_gather | solution.py:255
  7.9 132.4 %all-gather.5.cloned.1.call-start = ((), (), s32[]{:S(2)}) async-start(), calls=%async_computation.1 | async-start | bytes 4456448 | tf_op jit(solution)/shard_map/all_gather | solution.py:260
  9.8 7.1 %collective-permute-start.2 = (bf16[128,1024]{1,0:T(8,128)(2,1)S(1)}, bf16[128,1024]{1,0:T(8,128)(2,1)S(1)}, u32[]{:S(2)}, u32[]{:S(2)}) collective-permute-start(bf16[128,1024]{1,0:T(8,128)(2,1)S(1)} %constant_dynamic-update-slice_fusion), channel_id=1, source_target_pairs={{0,16},{1,65},{2,18},{3,67},{4,20},{5,69},{6,22},{7,71},{8,24},{9,... | collective-permute-start | bytes 786440 | tf_op jit(solution)/shard_map/ppermute | solution.py:29
  11.9 9.3 %collective-permute-start.1 = (bf16[128,1024]{1,0:T(8,128)(2,1)S(1)}, bf16[128,1024]{1,0:T(8,128)(2,1)S(1)}, u32[]{:S(2)}, u32[]{:S(2)}) collective-permute-start(bf16[128,1024]{1,0:T(8,128)(2,1)S(1)} %constant_dynamic-update-slice_fusion), channel_id=1, source_target_pairs={{0,32},{1,129},{2,34},{3,131},{4,36},{5,133},{6,38},{7,135},{8,40}... | collective-permute-start | bytes 786440 | tf_op jit(solution)/shard_map/ppermute | solution.py:29
  14.3 6.9 %collective-permute-start = (bf16[128,1024]{1,0:T(8,128)(2,1)S(1)}, bf16[128,1024]{1,0:T(8,128)(2,1)S(1)}, u32[]{:S(2)}, u32[]{:S(2)}) collective-permute-start(bf16[128,1024]{1,0:T(8,128)(2,1)S(1)} %constant_dynamic-update-slice_fusion), channel_id=1, source_target_pairs={{0,48},{1,193},{2,50},{3,195},{4,52},{5,197},{6,54},{7,199},{8,56}... | collective-permute-start | bytes 786440 | tf_op jit(solution)/shard_map/ppermute | solution.py:29
  22.3 15.8 %collective-permute-start.5 = (bf16[512,1024]{1,0:T(8,128)(2,1)}, bf16[512,1024]{1,0:T(8,128)(2,1)}, u32[]{:S(2)}, u32[]{:S(2)}) collective-permute-start(bf16[512,1024]{1,0:T(8,128)(2,1)} %pad_maximum_fusion.pre_ref), channel_id=1, source_target_pairs={{0,128},{1,33},{2,130},{3,35},{4,132},{5,37},{6,134},{7,39},{8,136... | collective-permute-start | bytes 3145736 | tf_op jit(solution)/shard_map/ppermute | solution.py:29
  24.9 24.3 %collective-permute-start.4 = (bf16[512,1024]{1,0:T(8,128)(2,1)}, bf16[512,1024]{1,0:T(8,128)(2,1)S(1)}, u32[]{:S(2)}, u32[]{:S(2)}) collective-permute-start(bf16[512,1024]{1,0:T(8,128)(2,1)} %pad_maximum_fusion.pre_ref), channel_id=1, source_target_pairs={{0,64},{1,17},{2,66},{3,19},{4,68},{5,21},{6,70},{7,23},{8,72},{9,... | collective-permute-start | bytes 3145736 | tf_op jit(solution)/shard_map/ppermute | solution.py:29
  25.3 25.8 %collective-permute-start.3 = (bf16[512,1024]{1,0:T(8,128)(2,1)}, bf16[512,1024]{1,0:T(8,128)(2,1)}, u32[]{:S(2)}, u32[]{:S(2)}) collective-permute-start(bf16[512,1024]{1,0:T(8,128)(2,1)} %pad_maximum_fusion.pre_ref), channel_id=1, source_target_pairs={{0,192},{1,49},{2,194},{3,51},{4,196},{5,53},{6,198},{7,55},{8,200... | collective-permute-start | bytes 3145736 | tf_op jit(solution)/shard_map/ppermute | solution.py:29
  60.0 13.7 %collective-permute-start.6 = (bf16[512,512]{1,0:T(8,128)(2,1)S(1)}, bf16[512,512]{1,0:T(8,128)(2,1)S(1)}, u32[]{:S(2)}, u32[]{:S(2)}) collective-permute-start(bf16[512,512]{1,0:T(8,128)(2,1)S(1)} %shard_map.179), channel_id=1, source_target_pairs={{0,128},{1,33},{2,130},{3,35},{4,132},{5,37},{6,134},{7,39},{8,136... | collective-permute-start | bytes 1572872 | tf_op jit(solution)/shard_map/ppermute | solution.py:29
  64.4 11.2 %collective-permute-start.7 = (bf16[512,512]{1,0:T(8,128)(2,1)S(1)}, bf16[512,512]{1,0:T(8,128)(2,1)S(1)}, u32[]{:S(2)}, u32[]{:S(2)}) collective-permute-start(bf16[512,512]{1,0:T(8,128)(2,1)S(1)} %shard_map.180), channel_id=1, source_target_pairs={{0,64},{1,17},{2,66},{3,19},{4,68},{5,21},{6,70},{7,23},{8,72},{9,... | collective-permute-start | bytes 1572872 | tf_op jit(solution)/shard_map/ppermute | solution.py:29
  66.6 9.1 %collective-permute-start.8 = (bf16[512,512]{1,0:T(8,128)(2,1)S(1)}, bf16[512,512]{1,0:T(8,128)(2,1)S(1)}, u32[]{:S(2)}, u32[]{:S(2)}) collective-permute-start(bf16[512,512]{1,0:T(8,128)(2,1)S(1)} %shard_map.181), channel_id=1, source_target_pairs={{0,192},{1,49},{2,194},{3,51},{4,196},{5,53},{6,198},{7,55},{8,200... | collective-permute-start | bytes 1572872 | tf_op jit(solution)/shard_map/ppermute | solution.py:29
  76.0 25.2 %copy-start.18 = (s32[4]{0:T(128)S(1)}, s32[4]{0:T(128)}, u32[]{:S(2)}) copy-start(s32[4]{0:T(128)} %constant.225.clone) | copy-start | bytes 52
  76.0 25.2 %copy-start.19 = (s32[4]{0:T(128)S(1)}, s32[4]{0:T(128)}, u32[]{:S(2)}) copy-start(s32[4]{0:T(128)} %constant.224.clone) | copy-start | bytes 52
  76.1 5.8 %collective-permute-start.11 = (f32[128,512]{1,0:T(8,128)S(1)}, f32[128,512]{1,0:T(8,128)S(1)}, u32[]{:S(2)}, u32[]{:S(2)}) collective-permute-start(f32[128,512]{1,0:T(8,128)S(1)} %get-tuple-element.71), channel_id=1, source_target_pairs={{0,48},{1,193},{2,50},{3,195},{4,52},{5,197},{6,54},{7,199},{8,56}... | collective-permute-start | bytes 786440 | tf_op jit(solution)/shard_map/ppermute | solution.py:29
  78.6 9.5 %collective-permute-start.10 = (f32[128,512]{1,0:T(8,128)S(1)}, f32[128,512]{1,0:T(8,128)S(1)}, u32[]{:S(2)}, u32[]{:S(2)}) collective-permute-start(f32[128,512]{1,0:T(8,128)S(1)} %get-tuple-element.72), channel_id=1, source_target_pairs={{0,16},{1,65},{2,18},{3,67},{4,20},{5,69},{6,22},{7,71},{8,24},{9,... | collective-permute-start | bytes 786440 | tf_op jit(solution)/shard_map/ppermute | solution.py:29
  78.6 9.5 %collective-permute-start.9 = (f32[128,512]{1,0:T(8,128)S(1)}, f32[128,512]{1,0:T(8,128)S(1)}, u32[]{:S(2)}, u32[]{:S(2)}) collective-permute-start(f32[128,512]{1,0:T(8,128)S(1)} %get-tuple-element.70), channel_id=1, source_target_pairs={{0,32},{1,129},{2,34},{3,131},{4,36},{5,133},{6,38},{7,135},{8,40}... | collective-permute-start | bytes 786440 | tf_op jit(solution)/shard_map/ppermute | solution.py:29
  88.2 6.9 %collective-permute-start.14 = (bf16[128,512]{1,0:T(8,128)(2,1)S(1)}, bf16[128,512]{1,0:T(8,128)(2,1)S(1)}, u32[]{:S(2)}, u32[]{:S(2)}) collective-permute-start(bf16[128,512]{1,0:T(8,128)(2,1)S(1)} %fusion.5), channel_id=1, source_target_pairs={{0,16},{1,65},{2,18},{3,67},{4,20},{5,69},{6,22},{7,71},{8,24},{9,... | collective-permute-start | bytes 393224 | tf_op jit(solution)/shard_map/ppermute | solution.py:29
  88.3 6.8 %collective-permute-start.13 = (bf16[128,512]{1,0:T(8,128)(2,1)S(1)}, bf16[128,512]{1,0:T(8,128)(2,1)S(1)}, u32[]{:S(2)}, u32[]{:S(2)}) collective-permute-start(bf16[128,512]{1,0:T(8,128)(2,1)S(1)} %fusion.5), channel_id=1, source_target_pairs={{0,32},{1,129},{2,34},{3,131},{4,36},{5,133},{6,38},{7,135},{8,40}... | collective-permute-start | bytes 393224 | tf_op jit(solution)/shard_map/ppermute | solution.py:29
  89.4 6.4 %collective-permute-start.12 = (bf16[128,512]{1,0:T(8,128)(2,1)S(1)}, bf16[128,512]{1,0:T(8,128)(2,1)S(1)}, u32[]{:S(2)}, u32[]{:S(2)}) collective-permute-start(bf16[128,512]{1,0:T(8,128)(2,1)S(1)} %fusion.5), channel_id=1, source_target_pairs={{0,48},{1,193},{2,50},{3,195},{4,52},{5,197},{6,54},{7,199},{8,56}... | collective-permute-start | bytes 393224 | tf_op jit(solution)/shard_map/ppermute | solution.py:29
  95.8 10.1 %collective-permute-start.17 = (bf16[512,512]{1,0:T(8,128)(2,1)S(1)}, bf16[512,512]{1,0:T(8,128)(2,1)}, u32[]{:S(2)}, u32[]{:S(2)}) collective-permute-start(bf16[512,512]{1,0:T(8,128)(2,1)S(1)} %pad_maximum_fusion.1.hidden_ref), channel_id=1, source_target_pairs={{0,128},{1,33},{2,130},{3,35},{4,132},{5,37},{6,134},{7,39},{8,136... | collective-permute-start | bytes 1572872 | tf_op jit(solution)/shard_map/ppermute | solution.py:29
  98.5 12.9 %collective-permute-start.16 = (bf16[512,512]{1,0:T(8,128)(2,1)S(1)}, bf16[512,512]{1,0:T(8,128)(2,1)}, u32[]{:S(2)}, u32[]{:S(2)}) collective-permute-start(bf16[512,512]{1,0:T(8,128)(2,1)S(1)} %pad_maximum_fusion.1.hidden_ref), channel_id=1, source_target_pairs={{0,64},{1,17},{2,66},{3,19},{4,68},{5,21},{6,70},{7,23},{8,72},{9,... | collective-permute-start | bytes 1572872 | tf_op jit(solution)/shard_map/ppermute | solution.py:29
  99.2 13.8 %collective-permute-start.15 = (bf16[512,512]{1,0:T(8,128)(2,1)S(1)}, bf16[512,512]{1,0:T(8,128)(2,1)S(1)}, u32[]{:S(2)}, u32[]{:S(2)}) collective-permute-start(bf16[512,512]{1,0:T(8,128)(2,1)S(1)} %pad_maximum_fusion.1.hidden_ref), channel_id=1, source_target_pairs={{0,192},{1,49},{2,194},{3,51},{4,196},{5,53},{6,198},{7,55},{8,200... | collective-permute-start | bytes 1572872 | tf_op jit(solution)/shard_map/ppermute | solution.py:29
  114.9 20.8 %copy-start.2 = (bf16[2048,512]{1,0:T(8,128)(2,1)}, bf16[2048,512]{1,0:T(8,128)(2,1)S(1)}, u32[]{:S(2)}) copy-start(bf16[2048,512]{1,0:T(8,128)(2,1)S(1)} %get-tuple-element.57.refs_3_.refs_4_) | copy-start | bytes 6291460
  117.1 9.7 %collective-permute-start.18 = (f32[512,1024]{1,0:T(8,128)S(1)}, f32[512,1024]{1,0:T(8,128)S(1)}, u32[]{:S(2)}, u32[]{:S(2)}) collective-permute-start(f32[512,1024]{1,0:T(8,128)S(1)} %shard_map.186), channel_id=1, source_target_pairs={{0,1},{1,0},{2,3},{3,2},{4,5},{5,4},{6,7},{7,6},{8,9},{9,8},{10,11... | collective-permute-start | bytes 6291464 | tf_op jit(solution)/shard_map/ppermute | solution.py:29
  124.7 11.0 %copy-start.12 = (s32[4]{0:T(128)S(1)}, s32[4]{0:T(128)}, u32[]{:S(2)}) copy-start(s32[4]{0:T(128)} %constant.231.clone) | copy-start | bytes 52
  124.7 11.0 %copy-start.13 = (s32[4]{0:T(128)S(1)}, s32[4]{0:T(128)}, u32[]{:S(2)}) copy-start(s32[4]{0:T(128)} %constant.230.clone) | copy-start | bytes 52
  126.8 11.6 %collective-permute-start.20 = (f32[512,1024]{1,0:T(8,128)S(1)}, f32[512,1024]{1,0:T(8,128)S(1)}, u32[]{:S(2)}, u32[]{:S(2)}) collective-permute-start(f32[512,1024]{1,0:T(8,128)S(1)} %shard_map.188), channel_id=1, source_target_pairs={{0,1},{1,0},{2,3},{3,2},{4,5},{5,4},{6,7},{7,6},{8,9},{9,8},{10,11... | collective-permute-start | bytes 6291464 | tf_op jit(solution)/shard_map/ppermute | solution.py:29
  127.0 13.3 %collective-permute-start.19 = (bf16[128,1024]{1,0:T(8,128)(2,1)S(1)}, bf16[128,1024]{1,0:T(8,128)(2,1)S(1)}, u32[]{:S(2)}, u32[]{:S(2)}) collective-permute-start(bf16[128,1024]{1,0:T(8,128)(2,1)S(1)} %add_convert_fusion.2), channel_id=1, source_target_pairs={{0,2},{1,15},{2,4},{3,1},{4,6},{5,3},{6,8},{7,5},{8,10},{9,7},{10,... | collective-permute-start | bytes 786440 | tf_op jit(solution)/shard_map/ppermute | solution.py:29
  141.5 8.4 %collective-permute-start.21 = (bf16[256,1024]{1,0:T(8,128)(2,1)S(1)}, bf16[256,1024]{1,0:T(8,128)(2,1)S(1)}, u32[]{:S(2)}, u32[]{:S(2)}) collective-permute-start(bf16[256,1024]{1,0:T(8,128)(2,1)S(1)} %pad_maximum_fusion.2), channel_id=1, source_target_pairs={{0,2},{1,15},{2,4},{3,1},{4,6},{5,3},{6,8},{7,5},{8,10},{9,7},{10,... | collective-permute-start | bytes 1572872 | tf_op jit(solution)/shard_map/ppermute | solution.py:29
  150.0 9.2 %collective-permute-start.22 = (bf16[256,1024]{1,0:T(8,128)(2,1)S(1)}, bf16[256,1024]{1,0:T(8,128)(2,1)S(1)}, u32[]{:S(2)}, u32[]{:S(2)}) collective-permute-start(bf16[256,1024]{1,0:T(8,128)(2,1)S(1)} %add_convert_fusion.1), channel_id=1, source_target_pairs={{0,2},{1,15},{2,4},{3,1},{4,6},{5,3},{6,8},{7,5},{8,10},{9,7},{10,... | collective-permute-start | bytes 1572872 | tf_op jit(solution)/shard_map/ppermute | solution.py:29
  159.4 9.3 %collective-permute-start.23 = (bf16[256,1024]{1,0:T(8,128)(2,1)S(1)}, bf16[256,1024]{1,0:T(8,128)(2,1)S(1)}, u32[]{:S(2)}, u32[]{:S(2)}) collective-permute-start(bf16[256,1024]{1,0:T(8,128)(2,1)S(1)} %add_convert_fusion), channel_id=1, source_target_pairs={{0,2},{1,15},{2,4},{3,1},{4,6},{5,3},{6,8},{7,5},{8,10},{9,7},{10,... | collective-permute-start | bytes 1572872 | tf_op jit(solution)/shard_map/ppermute | solution.py:29
  168.7 6.9 %collective-permute-start.24 = (f32[128,1024]{1,0:T(8,128)S(1)}, f32[128,1024]{1,0:T(8,128)S(1)}, u32[]{:S(2)}, u32[]{:S(2)}) collective-permute-start(f32[128,1024]{1,0:T(8,128)S(1)} %slice.77), channel_id=1, source_target_pairs={{0,1},{1,0},{2,3},{3,2},{4,5},{5,4},{6,7},{7,6},{8,9},{9,8},{10,11... | collective-permute-start | bytes 1572872 | tf_op jit(solution)/shard_map/ppermute | solution.py:29
  (15 other events, 64.9 us)
Sparse Core Ops, SparseCore 0:
  9.8 46.3 all-gather.2
  58.0 42.6 all-gather.4
